TPU v7x, 32 devices: a whole 2x2x4 slice. The times are simulated.
32 devices in a mesh: seq: 8 (over y, x, core), head: 4 (over z).
Axes of the slice: x: 2, y: 2, z: 4, core: 2. Of those that a mesh axis runs over, the one named last changes fastest.
Arguments:
- tokens: bfloat16 [2, 4096, 1024], P(None, 'seq'), may hold values from -6 to 6
- cotangent: bfloat16 [2, 4096, 1024], P(None, 'seq'), may hold values from -6 to 6
- doc_starts: int32 [2, 4], replicated, may hold values from 0 to 4096, as said below
- norm_gain: float32 [1024], replicated, may hold values from 0.5 to 1.5
- mixer_proj: bfloat16 [1024, 2, 1536], P(None, None, 'head'), may hold values from -0.1875 to 0.1875
- state_proj: bfloat16 [1024, 256], replicated, may hold values from -0.1875 to 0.1875
- step_proj: bfloat16 [1024, 24], P(None, 'head'), may hold values from -0.1875 to 0.1875
- step_bias: float32 [24], P('head'), may hold values from -2 to 0
- decay_log: float32 [24], P('head'), as said below
- skip_gain: float32 [24], P('head'), may hold values from 0.5 to 1.5
- conv_mixer: float32 [4, 1536], P(None, 'head'), may hold values from -3 to 3
- conv_state: float32 [4, 256], replicated, may hold values from -0.75 to 0.75
- mixer_down: bfloat16 [1536, 1024], P('head'), may hold values from -0.15625 to 0.15625
- query_proj: bfloat16 [1024, 512], P(None, 'head'), may hold values from -0.1875 to 0.1875
- keyval_proj: bfloat16 [1024, 2, 128], replicated, may hold values from -0.1875 to 0.1875
- attend_down: bfloat16 [512, 1024], P('head'), may hold values from -3 to 3
- ffn_gain: float32 [1024], replicated, may hold values from 0.5 to 1.5
- ffn_in: bfloat16 [1024, 2, 2048], P(None, None, 'head'), may hold values from -0.1875 to 0.1875
- ffn_down: bfloat16 [2048, 1024], P('head'), may hold values from -0.125 to 0.125
Outputs:
- output: bfloat16 [2, 4096, 1024], P(None, 'seq')
- token_grad: bfloat16 [2, 4096, 1024], P(None, 'seq')
- norm_gain_grad: float32 [1024], replicated
- mixer_proj_grad: float32 [1024, 2, 1536], P(None, None, 'head')
- state_proj_grad: float32 [1024, 256], replicated
- step_proj_grad: float32 [1024, 24], P(None, 'head')
- step_bias_grad: float32 [24], P('head')
- decay_log_grad: float32 [24], P('head')
- skip_gain_grad: float32 [24], P('head')
- conv_mixer_grad: float32 [4, 1536], P(None, 'head')
- conv_state_grad: float32 [4, 256], replicated
- mixer_down_grad: float32 [1536, 1024], P('head')
- query_proj_grad: float32 [1024, 512], P(None, 'head')
- keyval_proj_grad: float32 [1024, 2, 128], replicated
- attend_down_grad: float32 [512, 1024], P('head')
- ffn_gain_grad: float32 [1024], replicated
- ffn_in_grad: float32 [1024, 2, 2048], P(None, None, 'head')
- ffn_down_grad: float32 [2048, 1024], P('head')
Inputs may be any that keep to these rules, and one draw needn't show every extreme that they name: `doc_starts`: each row lists its documents' first places in rising order, the first 0; a start equal to 4096 is an empty document. In one row, drawn from the seed, a single document fills the whole row; the other rows hold 4 documents, none empty. `decay_log`: each head's value lies between ln(0.02 / 4096) and ln(1 / 16).
All inputs are finite; a program needn't handle non-finite values.
Results may differ from a plain program's by a relative error of at most 0.029.
Values may be sent and summed in bfloat16 or wider, within the bound.
A program may use at most 192 MiB of HBM per device.

v0:
```python
from functools import partial
import math

import jax
import jax.numpy as jnp
from jax import lax
from jax.sharding import PartitionSpec as P

ATT_HEADS = 8
KV_HEADS = 2
ATT_DIM = 64


EPSILON = 1e-05
PRECISE = lax.Precision.HIGHEST
ROPE_BASE = 10000.0
FLOOR_SCORE = -1e30


def shifted(block, axis, distance):
    devices = range(lax.axis_size(axis))
    route = [(i - distance, i) for i in devices if i - distance in devices]
    return lax.ppermute(block, axis, route)


def carried_in(shard, axis, combine, identity, reverse):
    size, index = (lax.axis_size(axis), lax.axis_index(axis))
    everything = jax.tree.map(
        lambda part, kind: lax.all_gather(part.astype(kind), axis),
        shard,
        (jnp.bfloat16, jnp.bfloat16),
    )
    start = jax.tree.map(
        lambda part, zero: jnp.broadcast_to(jnp.asarray(zero, part.dtype), part.shape),
        shard,
        identity,
    )

    def turn(k, before):
        at = size - 1 - k if reverse else k
        reached = at > index if reverse else at < index
        new = combine(
            before, jax.tree.map(lambda part, own: part[at].astype(own.dtype), everything, shard)
        )
        return jax.tree.map(lambda a, b: jnp.where(reached, a, b), new, before)

    return lax.fori_loop(0, size, turn, start)


def silu_value(values):
    return values * jax.nn.sigmoid(values)


def silu_slope(values):
    logistic = jax.nn.sigmoid(values)
    return logistic * (1.0 + values * (1.0 - logistic))


def doc_layout(starts, offset, length):
    places = offset + jnp.arange(length, dtype=jnp.int32)
    passed = starts[:, None, :] <= places[None, :, None]
    doc_ids = jnp.sum(passed.astype(jnp.int32), axis=2)
    begins = jnp.max(jnp.where(passed, starts[:, None, :], 0), axis=2)
    return (doc_ids, places[None, :] - begins)


def rotate(values, positions, signed):
    half_dim = values.shape[-1] // 2
    inv_freq = jnp.exp(
        jnp.arange(half_dim).astype(jnp.float32) * (-2.0 * math.log(ROPE_BASE) / values.shape[-1])
    )
    angles = positions.astype(jnp.float32)[:, :, None] * inv_freq
    cosine = jnp.cos(angles)[:, :, None, :]
    sine_part = signed * jnp.sin(angles)[:, :, None, :]
    front_half = values[..., :half_dim]
    back_half = values[..., half_dim:]
    return jnp.concatenate(
        [front_half * cosine - back_half * sine_part, back_half * cosine + front_half * sine_part],
        axis=-1,
    )


def norm_forward(values, gain_vec):
    scaled = lax.rsqrt(jnp.mean(values * values, axis=-1, keepdims=True) + EPSILON)
    normed = values * scaled
    return (normed, scaled, normed * gain_vec)


def norm_backward(upstream, normed, scaled, gain_vec):
    inner_grad = upstream * gain_vec
    back_grad = scaled * (
        inner_grad - normed * jnp.mean(inner_grad * normed, axis=-1, keepdims=True)
    )
    return (back_grad, jnp.sum(upstream * normed, axis=(0, 1)))


def state_summary(doc_ids, positions, inner_act, b_vec, step_size, log_keep):
    piece_len = inner_act.shape[1]
    cum_keep = jnp.cumsum(log_keep, axis=1)
    drive_in = inner_act * step_size[..., None]
    tail_rate = jnp.where(
        (doc_ids == doc_ids[:, -1:])[:, :, None], jnp.exp(cum_keep[:, -1:, :] - cum_keep), 0.0
    )
    fresh_state = jnp.einsum("rsh,rshp,rsn->rhpn", tail_rate, drive_in, b_vec, precision=PRECISE)
    keep_rate = jnp.where(positions[:, -1:] > piece_len - 1, jnp.exp(cum_keep[:, -1]), 0.0)
    return (fresh_state, keep_rate)


def state_output(doc_ids, positions, inner_act, b_vec, c_vec, step_size, log_keep, entering):
    piece_len = inner_act.shape[1]
    local_place = jnp.arange(piece_len, dtype=jnp.int32)
    cum_keep = jnp.cumsum(log_keep, axis=1)
    causal_mask = (local_place[:, None] >= local_place[None, :])[None] & (
        doc_ids[:, :, None] == doc_ids[:, None, :]
    )
    gap_log = cum_keep[:, :, None, :] - cum_keep[:, None, :, :]
    decay_mat = jnp.where(
        causal_mask[..., None], jnp.exp(jnp.where(causal_mask[..., None], gap_log, 0.0)), 0.0
    )
    gram_mat = jnp.einsum("rtn,rsn->rts", c_vec, b_vec, precision=PRECISE)
    drive_in = inner_act * step_size[..., None]
    state_out = jnp.einsum(
        "rtsh,rshp->rthp", gram_mat[..., None] * decay_mat, drive_in, precision=PRECISE
    )
    lift_rate = jnp.where((positions > local_place)[:, :, None], jnp.exp(cum_keep), 0.0)
    return (
        state_out
        + jnp.einsum("rtn,rhpn->rthp", c_vec, entering, precision=PRECISE) * lift_rate[..., None]
    )


def carry_forward(earlier, later):
    keep_early, state_early = earlier
    keep_late, state_late = later
    return (keep_early * keep_late, keep_late[..., None, None] * state_early + state_late)


def carry_backward(earlier, later):
    keep_early, grad_early = earlier
    keep_late, grad_late = later
    return (keep_late * keep_early, grad_late + keep_late[..., None, None] * grad_early)


def score_block(queries, key_piece, key_places, key_docs, query_places, query_docs, score_scale):
    raw_scores = (
        jnp.einsum("rthd,rsd->rhts", queries, key_piece, preferred_element_type=jnp.float32)
        * score_scale
    )
    allowed = (key_places[None, None, :] <= query_places[:, :, None]) & (
        key_docs[:, None, :] == query_docs[:, :, None]
    )
    return (raw_scores, allowed[:, None])


def block_probs(raw_scores, allowed, row_top, row_total):
    return jnp.where(allowed, jnp.exp(raw_scores - row_top[..., None]) / row_total[..., None], 0.0)


def local(
    tokens,
    cotangent,
    doc_starts,
    norm_gain,
    mixer_proj,
    state_proj,
    step_proj,
    step_bias,
    decay_log,
    skip_gain,
    conv_mixer,
    conv_state,
    mixer_down,
    query_proj,
    keyval_proj,
    attend_down,
    ffn_gain,
    ffn_in,
    ffn_down,
):
    row_count, length, model_width = tokens.shape
    seq_count = lax.axis_size("seq")
    offset = lax.axis_index("seq") * length
    head_ways = lax.axis_size("head")
    share_len = length // head_ways
    share_start = lax.axis_index("head") * share_len
    inner_width = mixer_proj.shape[2]
    head_count = step_bias.shape[0]
    head_dim = inner_width // head_count
    states = state_proj.shape[1] // 2
    tap_count = conv_mixer.shape[0]
    local_heads = query_proj.shape[1] // ATT_DIM
    kv_total = keyval_proj.shape[2] // ATT_DIM
    group_size = ATT_HEADS // KV_HEADS
    kv_index = lax.axis_index("head") * local_heads // group_size
    score_scale = ATT_DIM ** (-0.5)
    doc_ids, positions = doc_layout(doc_starts, offset, length)
    places = jnp.arange(length, dtype=jnp.int32)

    def share_of(values):
        return lax.dynamic_slice_in_dim(values, share_start, share_len, 1)

    inputs = tokens.astype(jnp.float32)
    normed_one, scaled_one, gained_one = norm_forward(inputs, norm_gain)
    normed_low = gained_one.astype(jnp.bfloat16)
    mixer_pre = jnp.einsum(
        "rtd,dkc->rtkc", normed_low, mixer_proj, preferred_element_type=jnp.float32
    )
    gate_view = mixer_pre[:, :, 0].reshape(row_count, length, head_count, head_dim)
    state_pre = jnp.einsum(
        "rtd,dc->rtc", normed_low, state_proj, preferred_element_type=jnp.float32
    )
    step_pre = jnp.einsum("rtd,dh->rth", normed_low, step_proj, preferred_element_type=jnp.float32)
    query_pre = jnp.einsum(
        "rtd,dc->rtc", normed_low, query_proj, preferred_element_type=jnp.float32
    )
    keyval_mine = lax.dynamic_slice_in_dim(keyval_proj, kv_index * ATT_DIM, ATT_DIM, 2)
    keyval_pre = jnp.einsum(
        "rtd,dkc->rtkc", normed_low, keyval_mine, preferred_element_type=jnp.float32
    )
    conv_input = jnp.concatenate([mixer_pre[:, :, 1], state_pre], axis=2).astype(jnp.bfloat16)
    conv_weight = jnp.concatenate([conv_mixer, conv_state], axis=1)
    before = shifted(conv_input[:, length - (tap_count - 1) :], "seq", 1)
    padded = jnp.concatenate([before, conv_input], axis=1)
    conv_pre = jnp.zeros(conv_input.shape, jnp.float32)
    for tap_index in range(tap_count):
        lag_steps = tap_count - 1 - tap_index
        conv_pre = conv_pre + jnp.where(
            (positions >= lag_steps)[:, :, None],
            padded[:, tap_index : tap_index + length] * conv_weight[tap_index],
            0.0,
        )
    activated = silu_value(conv_pre).astype(jnp.bfloat16)
    mixer_act = (
        activated[:, :, :inner_width]
        .reshape(row_count, length, head_count, head_dim)
        .astype(jnp.float32)
    )
    state_b = activated[:, :, inner_width : inner_width + states].astype(jnp.float32)
    state_c = activated[:, :, inner_width + states :].astype(jnp.float32)
    step_size = jax.nn.softplus(step_pre + step_bias)
    decay_rates = jnp.exp(decay_log)
    log_keep = -step_size * decay_rates
    (fresh_state, keep_rate), summary_back = jax.vjp(
        partial(state_summary, doc_ids, positions), mixer_act, state_b, step_size, log_keep
    )
    chain_keep, entering = carried_in(
        (keep_rate, fresh_state),
        "seq",
        carry_forward,
        (jnp.ones_like(keep_rate), jnp.zeros_like(fresh_state)),
        False,
    )
    mixed_state, output_back = jax.vjp(
        partial(state_output, doc_ids, positions),
        mixer_act,
        state_b,
        state_c,
        step_size,
        log_keep,
        entering,
    )
    full_state = mixed_state + skip_gain[:, None] * mixer_act
    gated_low = (
        (full_state * silu_value(gate_view))
        .reshape(row_count, length, inner_width)
        .astype(jnp.bfloat16)
    )
    mixer_part = jnp.einsum(
        "rtc,cd->rtd", gated_low, mixer_down, preferred_element_type=jnp.float32
    )
    query_rot = rotate(
        query_pre.reshape(row_count, length, local_heads, ATT_DIM), positions, 1.0
    ).astype(jnp.bfloat16)
    key_rot = rotate(keyval_pre[:, :, 0][:, :, None], positions, 1.0)[:, :, 0].astype(jnp.bfloat16)
    value_low = keyval_pre[:, :, 1].astype(jnp.bfloat16)
    all_keys, all_values = (
        lax.all_gather(key_rot, "seq", axis=1, tiled=True),
        lax.all_gather(value_low, "seq", axis=1, tiled=True),
    )
    full_len = all_keys.shape[1]
    key_docs = doc_layout(doc_starts, 0, full_len)[0]
    per_block = math.gcd(seq_count, max(1, 512 // length))
    block_span = length * per_block
    block_total = full_len // block_span
    query_places = (offset + places)[None, :]

    def key_piece_at(block_start):
        key_piece = lax.dynamic_slice_in_dim(all_keys, block_start, block_span, 1)
        value_piece = lax.dynamic_slice_in_dim(all_values, block_start, block_span, 1)
        doc_piece = lax.dynamic_slice_in_dim(key_docs, block_start, block_span, 1)
        key_places = block_start + jnp.arange(block_span, dtype=jnp.int32)
        return (key_piece, value_piece, doc_piece, key_places)

    def stats_step(block_index, loop_carry):
        row_top, row_total = loop_carry
        key_piece, value_piece, doc_piece, key_places = key_piece_at(block_index * block_span)
        raw_scores, allowed = score_block(
            query_rot, key_piece, key_places, doc_piece, query_places, doc_ids, score_scale
        )
        masked = jnp.where(allowed, raw_scores, FLOOR_SCORE)
        new_top = jnp.maximum(row_top, jnp.max(masked, axis=-1))
        row_total = row_total * jnp.exp(row_top - new_top) + jnp.sum(
            jnp.where(allowed, jnp.exp(masked - new_top[..., None]), 0.0), axis=-1
        )
        return (new_top, row_total)

    stat_shape = (row_count, local_heads, length)
    row_top, row_total = lax.fori_loop(
        0,
        block_total,
        stats_step,
        (jnp.full(stat_shape, FLOOR_SCORE, jnp.float32), jnp.zeros(stat_shape, jnp.float32)),
    )

    def value_step(block_index, attend_acc):
        key_piece, value_piece, doc_piece, key_places = key_piece_at(block_index * block_span)
        raw_scores, allowed = score_block(
            query_rot, key_piece, key_places, doc_piece, query_places, doc_ids, score_scale
        )
        probs_low = block_probs(raw_scores, allowed, row_top, row_total).astype(jnp.bfloat16)
        return attend_acc + jnp.einsum(
            "rhts,rsd->rthd", probs_low, value_piece, preferred_element_type=jnp.float32
        )

    attended = lax.fori_loop(
        0,
        block_total,
        value_step,
        jnp.zeros((row_count, length, local_heads, ATT_DIM), jnp.float32),
    )
    attended_low = attended.astype(jnp.bfloat16).reshape(row_count, length, local_heads * ATT_DIM)
    attend_part = jnp.einsum(
        "rtc,cd->rtd", attended_low, attend_down, preferred_element_type=jnp.float32
    )
    mixed_sum = lax.psum((mixer_part + attend_part).astype(jnp.bfloat16), "head").astype(
        jnp.float32
    )
    middle = inputs + mixed_sum
    normed_two, scaled_two, gained_two = norm_forward(middle, ffn_gain)
    middle_low = gained_two.astype(jnp.bfloat16)
    ffn_pre = jnp.einsum("rtd,dkf->rtkf", middle_low, ffn_in, preferred_element_type=jnp.float32)
    hidden = (silu_value(ffn_pre[:, :, 0]) * ffn_pre[:, :, 1]).astype(jnp.bfloat16)
    ffn_part = jnp.einsum("rtf,fd->rtd", hidden, ffn_down, preferred_element_type=jnp.float32)
    ffn_share_sum = lax.psum_scatter(
        ffn_part.astype(jnp.bfloat16), "head", scatter_dimension=1, tiled=True
    ).astype(jnp.float32)
    output_share = (share_of(middle) + ffn_share_sum).astype(jnp.bfloat16)
    hidden_grad = jnp.einsum("rtd,fd->rtf", cotangent, ffn_down, preferred_element_type=jnp.float32)
    ffn_down_grad = jnp.einsum("rtf,rtd->fd", hidden, cotangent, preferred_element_type=jnp.float32)
    gate_value = ffn_pre[:, :, 0]
    ffn_pre_grad = jnp.stack(
        [
            hidden_grad * ffn_pre[:, :, 1] * silu_slope(gate_value),
            hidden_grad * silu_value(gate_value),
        ],
        axis=2,
    ).astype(jnp.bfloat16)
    ffn_in_grad = jnp.einsum(
        "rtd,rtkf->dkf", middle_low, ffn_pre_grad, preferred_element_type=jnp.float32
    )
    middle_low_part = jnp.einsum(
        "rtkf,dkf->rtd", ffn_pre_grad, ffn_in, preferred_element_type=jnp.float32
    )
    low_grad_share = lax.psum_scatter(
        middle_low_part.astype(jnp.bfloat16), "head", scatter_dimension=1, tiled=True
    ).astype(jnp.float32)
    norm_back_share, ffn_gain_part = norm_backward(
        low_grad_share, share_of(normed_two), share_of(scaled_two), ffn_gain
    )
    middle_grad_share = share_of(cotangent).astype(jnp.float32) + norm_back_share
    mixed_low = lax.all_gather(middle_grad_share.astype(jnp.bfloat16), "head", axis=1, tiled=True)
    gated_grad = jnp.einsum(
        "rtd,cd->rtc", mixed_low, mixer_down, preferred_element_type=jnp.float32
    ).reshape(row_count, length, head_count, head_dim)
    mixer_down_grad = jnp.einsum(
        "rtc,rtd->cd", gated_low, mixed_low, preferred_element_type=jnp.float32
    )
    attended_grad = jnp.einsum(
        "rtd,cd->rtc", mixed_low, attend_down, preferred_element_type=jnp.float32
    ).astype(jnp.bfloat16)
    attend_down_grad = jnp.einsum(
        "rtc,rtd->cd", attended_low, mixed_low, preferred_element_type=jnp.float32
    )
    attended_grad = attended_grad.reshape(row_count, length, local_heads, ATT_DIM)
    grad_dot = jnp.swapaxes(jnp.sum(attended_grad.astype(jnp.float32) * attended, axis=-1), 1, 2)

    def query_side(block_start):
        key_piece, value_piece, doc_piece, key_places = key_piece_at(block_start)
        raw_scores, allowed = score_block(
            query_rot, key_piece, key_places, doc_piece, query_places, doc_ids, score_scale
        )
        soft_probs = block_probs(raw_scores, allowed, row_top, row_total)
        prob_grad = jnp.einsum(
            "rthd,rsd->rhts", attended_grad, value_piece, preferred_element_type=jnp.float32
        )
        score_grad = (soft_probs * (prob_grad - grad_dot[..., None])).astype(jnp.bfloat16)
        return (soft_probs, score_grad, key_piece)

    query_zero = jnp.zeros((row_count, length, local_heads, ATT_DIM), jnp.float32)

    def reduce_step(block_index, loop_carry):
        query_grad, key_grads, value_grads = loop_carry
        block_start = block_index * block_span
        soft_probs, score_grad, key_piece = query_side(block_start)
        query_grad = (
            query_grad
            + jnp.einsum(
                "rhts,rsd->rthd", score_grad, key_piece, preferred_element_type=jnp.float32
            )
            * score_scale
        )
        key_block = (
            jnp.einsum("rhts,rthd->rsd", score_grad, query_rot, preferred_element_type=jnp.float32)
            * score_scale
        )
        value_block = jnp.einsum(
            "rhts,rthd->rsd",
            soft_probs.astype(jnp.bfloat16),
            attended_grad,
            preferred_element_type=jnp.float32,
        )
        key_grads = lax.dynamic_update_slice_in_dim(key_grads, key_block, block_start, 1)
        value_grads = lax.dynamic_update_slice_in_dim(value_grads, value_block, block_start, 1)
        return (query_grad, key_grads, value_grads)

    full_zero = jnp.zeros((row_count, full_len, ATT_DIM), jnp.float32)
    query_grad, key_grads, value_grads = lax.fori_loop(
        0, block_total, reduce_step, (query_zero, full_zero, full_zero)
    )
    key_grad, value_grad = (
        lax.psum_scatter(
            key_grads.astype(jnp.bfloat16), "seq", scatter_dimension=1, tiled=True
        ).astype(jnp.float32),
        lax.psum_scatter(
            value_grads.astype(jnp.bfloat16), "seq", scatter_dimension=1, tiled=True
        ).astype(jnp.float32),
    )
    query_low = (
        rotate(query_grad, positions, -1.0)
        .reshape(row_count, length, local_heads * ATT_DIM)
        .astype(jnp.bfloat16)
    )
    keyval_own = jnp.stack(
        [rotate(key_grad[:, :, None], positions, -1.0)[:, :, 0], value_grad], axis=2
    )
    keyval_part = jnp.zeros((row_count, length, 2, kv_total, ATT_DIM), jnp.float32)
    keyval_part = lax.dynamic_update_slice_in_dim(
        keyval_part, keyval_own[:, :, :, None], kv_index, 3
    )
    state_grad = gated_grad * silu_value(gate_view)
    gate_grad = gated_grad * full_state * silu_slope(gate_view)
    skip_gain_grad = jnp.sum(state_grad * mixer_act, axis=(0, 1, 3))
    lift_rate = jnp.where(
        (positions > places)[:, :, None], jnp.exp(jnp.cumsum(log_keep, axis=1)), 0.0
    )
    local_grad = jnp.einsum(
        "rthp,rtn->rhpn", state_grad * lift_rate[..., None], state_c, precision=PRECISE
    )
    chain_back, after_grad = carried_in(
        (keep_rate, local_grad),
        "seq",
        carry_backward,
        (jnp.ones_like(keep_rate), jnp.zeros_like(local_grad)),
        True,
    )
    keep_grad = jnp.sum(after_grad * entering, axis=(2, 3))
    act_grad_one, b_grad_one, step_grad_one, log_grad_one = summary_back((after_grad, keep_grad))
    act_grad_two, b_grad_two, c_grad, step_grad_two, log_grad_two, entering_grad = output_back(
        state_grad
    )
    mixer_act_grad = act_grad_one + act_grad_two + state_grad * skip_gain[:, None]
    log_grad = log_grad_one + log_grad_two
    step_grad = step_grad_one + step_grad_two - log_grad * decay_rates
    decay_log_grad = jnp.sum(log_grad * log_keep, axis=(0, 1))
    step_pre_grad = step_grad * jax.nn.sigmoid(step_pre + step_bias)
    step_bias_grad = jnp.sum(step_pre_grad, axis=(0, 1))
    step_low = step_pre_grad.astype(jnp.bfloat16)
    act_grad = jnp.concatenate(
        [mixer_act_grad.reshape(row_count, length, inner_width), b_grad_one + b_grad_two, c_grad],
        axis=2,
    )
    pre_grad = act_grad * silu_slope(conv_pre)
    state_total, keyval_total = (
        lax.psum(pre_grad[:, :, inner_width:].astype(jnp.bfloat16), "head").astype(jnp.float32),
        lax.psum(keyval_part.astype(jnp.bfloat16), "head").astype(jnp.float32),
    )
    pre_grad = jnp.concatenate([pre_grad[:, :, :inner_width], state_total], axis=2)
    padded_grad = jnp.zeros((row_count, length + tap_count - 1, pre_grad.shape[2]), jnp.float32)
    conv_grads = []
    for tap_index in range(tap_count):
        lag_steps = tap_count - 1 - tap_index
        masked = jnp.where((positions >= lag_steps)[:, :, None], pre_grad, 0.0)
        conv_grads.append(jnp.sum(masked * padded[:, tap_index : tap_index + length], axis=(0, 1)))
        padded_grad = padded_grad.at[:, tap_index : tap_index + length].add(
            masked * conv_weight[tap_index]
        )
    conv_weight_grad = jnp.stack(conv_grads, axis=0)
    rim_grad = shifted(padded_grad[:, : tap_count - 1], "seq", -1)
    conv_input_grad = padded_grad[:, tap_count - 1 :] + jnp.pad(
        rim_grad, ((0, 0), (length - (tap_count - 1), 0), (0, 0))
    )
    mixer_low = jnp.stack(
        [gate_grad.reshape(row_count, length, inner_width), conv_input_grad[:, :, :inner_width]],
        axis=2,
    ).astype(jnp.bfloat16)
    state_low = conv_input_grad[:, :, inner_width:].astype(jnp.bfloat16)
    keyval_low = keyval_total.reshape(row_count, length, 2, kv_total * ATT_DIM).astype(jnp.bfloat16)
    mixer_proj_grad = jnp.einsum(
        "rtd,rtkc->dkc", normed_low, mixer_low, preferred_element_type=jnp.float32
    )
    state_proj_grad = jnp.einsum(
        "rtd,rtc->dc", normed_low, state_low, preferred_element_type=jnp.float32
    )
    step_proj_grad = jnp.einsum(
        "rtd,rth->dh", normed_low, step_low, preferred_element_type=jnp.float32
    )
    query_proj_grad = jnp.einsum(
        "rtd,rtc->dc", normed_low, query_low, preferred_element_type=jnp.float32
    )
    keyval_proj_grad = jnp.einsum(
        "rtd,rtkc->dkc", normed_low, keyval_low, preferred_element_type=jnp.float32
    )
    head_part = (
        jnp.einsum("rtkc,dkc->rtd", mixer_low, mixer_proj, preferred_element_type=jnp.float32)
        + jnp.einsum("rth,dh->rtd", step_low, step_proj, preferred_element_type=jnp.float32)
        + jnp.einsum("rtc,dc->rtd", query_low, query_proj, preferred_element_type=jnp.float32)
    )
    common_share = jnp.einsum(
        "rtc,dc->rtd", share_of(state_low), state_proj, preferred_element_type=jnp.float32
    ) + jnp.einsum(
        "rtkc,dkc->rtd", share_of(keyval_low), keyval_proj, preferred_element_type=jnp.float32
    )
    normed_share = share_of(normed_one)
    norm_rider = jnp.sum(head_part * normed_one, axis=(0, 1)) + jnp.sum(
        common_share * normed_share, axis=(0, 1)
    )
    head_share, ffn_gain_total, norm_gain_total = (
        lax.psum_scatter(
            head_part.astype(jnp.bfloat16), "head", scatter_dimension=1, tiled=True
        ).astype(jnp.float32),
        lax.psum_scatter(
            jnp.broadcast_to(ffn_gain_part[None, None, :], (1, head_ways, model_width)).astype(
                jnp.bfloat16
            ),
            "head",
            scatter_dimension=1,
            tiled=True,
        ).astype(jnp.float32),
        lax.psum_scatter(
            jnp.broadcast_to(norm_rider[None, None, :], (1, head_ways, model_width)).astype(
                jnp.bfloat16
            ),
            "head",
            scatter_dimension=1,
            tiled=True,
        ).astype(jnp.float32),
    )
    ffn_gain_grad = ffn_gain_total.reshape(model_width)
    norm_gain_grad = norm_gain_total.reshape(model_width)
    norm_back_share_one, unused_gain = norm_backward(
        head_share + common_share, normed_share, share_of(scaled_one), norm_gain
    )
    token_share = (middle_grad_share + norm_back_share_one).astype(jnp.bfloat16)
    output, token_grad = (
        lax.all_gather(output_share, "head", axis=1, tiled=True),
        lax.all_gather(token_share, "head", axis=1, tiled=True),
    )
    (
        norm_gain_sum,
        mixer_proj_sum,
        state_proj_sum,
        step_proj_sum,
        step_bias_sum,
        decay_log_sum,
        skip_gain_sum,
        conv_mixer_sum,
        conv_state_sum,
        mixer_down_sum,
        query_proj_sum,
        keyval_proj_sum,
        attend_down_sum,
        ffn_gain_sum,
        ffn_in_sum,
        ffn_down_sum,
    ) = (
        lax.psum(norm_gain_grad.astype(jnp.bfloat16), "seq").astype(jnp.float32),
        lax.psum(mixer_proj_grad.astype(jnp.bfloat16), "seq").astype(jnp.float32),
        lax.psum(state_proj_grad.astype(jnp.bfloat16), "seq").astype(jnp.float32),
        lax.psum(step_proj_grad.astype(jnp.bfloat16), "seq").astype(jnp.float32),
        lax.psum(step_bias_grad.astype(jnp.bfloat16), "seq").astype(jnp.float32),
        lax.psum(decay_log_grad.astype(jnp.bfloat16), "seq").astype(jnp.float32),
        lax.psum(skip_gain_grad.astype(jnp.bfloat16), "seq").astype(jnp.float32),
        lax.psum(conv_weight_grad[:, :inner_width].astype(jnp.bfloat16), "seq").astype(jnp.float32),
        lax.psum(conv_weight_grad[:, inner_width:].astype(jnp.bfloat16), "seq").astype(jnp.float32),
        lax.psum(mixer_down_grad.astype(jnp.bfloat16), "seq").astype(jnp.float32),
        lax.psum(query_proj_grad.astype(jnp.bfloat16), "seq").astype(jnp.float32),
        lax.psum(keyval_proj_grad.astype(jnp.bfloat16), "seq").astype(jnp.float32),
        lax.psum(attend_down_grad.astype(jnp.bfloat16), "seq").astype(jnp.float32),
        lax.psum(ffn_gain_grad.astype(jnp.bfloat16), "seq").astype(jnp.float32),
        lax.psum(ffn_in_grad.astype(jnp.bfloat16), "seq").astype(jnp.float32),
        lax.psum(ffn_down_grad.astype(jnp.bfloat16), "seq").astype(jnp.float32),
    )
    return (
        output,
        token_grad,
        norm_gain_sum,
        mixer_proj_sum,
        state_proj_sum,
        step_proj_sum,
        step_bias_sum,
        decay_log_sum,
        skip_gain_sum,
        conv_mixer_sum,
        conv_state_sum,
        mixer_down_sum,
        query_proj_sum,
        keyval_proj_sum,
        attend_down_sum,
        ffn_gain_sum,
        ffn_in_sum,
        ffn_down_sum,
    )


def solution(mesh):
    placed = (
        P(None, "seq", None),
        P(None, "seq", None),
        P(),
        P(),
        P(None, None, "head"),
        P(),
        P(None, "head"),
        P("head"),
        P("head"),
        P("head"),
        P(None, "head"),
        P(),
        P("head", None),
        P(None, "head"),
        P(),
        P("head", None),
        P(),
        P(None, None, "head"),
        P("head", None),
    )
    return jax.shard_map(
        local,
        mesh=mesh,
        in_specs=placed,
        out_specs=(
            P(None, "seq", None),
            P(None, "seq", None),
            P(),
            P(None, None, "head"),
            P(),
            P(None, "head"),
            P("head"),
            P("head"),
            P("head"),
            P(None, "head"),
            P(),
            P("head", None),
            P(None, "head"),
            P(),
            P("head", None),
            P(),
            P(None, None, "head"),
            P("head", None),
        ),
        check_vma=False,
    )
```

profile of v0, /device:TPU:0, one launch (start us, length us, event | category | flops | bytes accessed | tf_op | source)
XLA Modules:
  0.0 1031.0 jit_solution(1513849473525894086)
XLA Ops:
  17.3 4.9 copy.232
  44.3 7.2 reduce-window.20
  68.9 9.9 all_gather.33
  83.6 4.6 multiply_convert_fusion.2
  94.3 41.3 %while.83 = (s32[]{:T(128)}, f32[2,2,512]{2,1,0:T(2,128)S(1)}, f32[2,2,512]{2,1,0:T(2,128)}, s32[2,4096]{1,0:T(2,128)}, s32[2,512]{1,0:T(2,128)S(1)}, /*index=5*...) while((s32[]{:T(128)}, f32[2,2,512]{2,1,0:T(2,128)S(1)}, ...), condition=%wide.region_11.12_spmd.clone, body=%wide.region_8.11_spmd.clone.sunk | while | flops 143928320 | bytes 11075838 | solution.py:308
  135.6 47.4 %while.84 = (s32[]{:T(128)}, f32[2,512,2,64]{1,3,2,0:T(8,128)}, bf16[2,4096,64]{1,2,0:T(8,128)(2,1)}, s32[2,4096]{1,0:T(2,128)}, s32[2,512]{1,0:T(2,128)S(1)}, /...) while((s32[]{:T(128)}, f32[2,512,2,64]{1,3,2,0:T(8,128)}, ...), condition=%wide.region_13.14_spmd.clone, body=%wide.region_12.13_spmd.clone.sunk | while | flops 275252224 | bytes 3188432 | solution.py:325
  188.6 13.6 %while.82 = (s32[]{:T(128)}, f32[2,6,64,128]{3,2,1,0:T(8,128)S(1)}, s32[]{:T(128)}, bf16[8,2,6]{2,1,0:T(2,128)(2,1)}, bf16[8,2,6,64,128]{4,3,2,1,0:T(8,128)(2,1)}, /*index=5*/s32[]{:T(128)}, s32[]{:T(128)}) while((s32[]{:T(128)}, f32[2,6,64,128]{3,2,1,0:T(8,128)S(1)}, s32[]{:T(128)}, bf16[8,2,6]{2,1,0:T(2,128)(2,1)}, ...), condition=%wide.region_6.7_spmd.clone, body=%wide.region_5.6_spmd.clone.sunk | while | flops 491536 | bytes 983273 | solution.py:47
  204.2 17.6 %multiply_convert_fusion.7 = (bf16[2,512,6,64]{1,3,2,0:T(8,128)(2,1)S(1)}, f32[2,512,6,64]{1,3,2,0:T(8,128)}) fusion(f32[2,512,6,64]{1,3,2,0:T(8,128)} %bitcast.512, f32[2,512,6,64]{1,3,2,0:T(8,128)S(1)} %bitcast.507, f32[6]{0:T(128)S(1)} %copy-done.139, f32[2,512,6,64]{1,3,2,0:T(8,128)S(1)} %fusion.195, f32[2,512,6]{1,2,0:T(8,128)S(1)} %copy-done.83, ...), kind=kOutput, calls=%fused_computation.195 | convolution fusion | flops 2432827392 | bytes 9773080 | tf_op jit(solution)/shard_map/jvp(rtsh,rshp->rthp)/dot_general | solution.py:122
  225.8 86.9 %all-reduce.14.cloned.1.call-done = bf16[2,512,1024]{2,1,0:T(8,128)(2,1)} async-done(((bf16[2,512,1024]{2,1,0:T(8,128)(2,1)}), bf16[2,512,1024]{2,1,0:T(8,128)(2,1)}) %all-reduce.14.cloned.1.call-update) | async-done | bytes 2097168 | tf_op jit(solution)/shard_map/psum | solution.py:335
  312.7 4.4 convert_add_fusion.2
  331.4 41.6 %reduce-scatter.10.cloned.1.call-done = bf16[2,128,1024]{2,1,0:T(8,128)(2,1)} async-done(((bf16[2,512,1024]{2,1,0:T(8,128)(2,1)}), bf16[2,128,1024]{2,1,0:T(8,128)(2,1)}) %reduce-scatter.10.cloned.1.call-update) | async-done | bytes 524304 | tf_op jit(solution)/shard_map/reduce_scatter | solution.py:364
  378.5 45.2 %all-gather.14.cloned.1.call-done = bf16[2,512,1024]{2,1,0:T(8,128)(2,1)} async-done(((bf16[2,128,1024]{2,1,0:T(8,128)(2,1)}), bf16[2,512,1024]{2,1,0:T(8,128)(2,1)}) %all-gather.14.cloned.1.call-update) | async-done | bytes 2097168 | tf_op jit(solution)/shard_map/all_gather | solution.py:371
  428.4 77.6 %while.86 = (s32[]{:T(128)}, f32[2,512,2,64]{1,3,2,0:T(8,128)S(1)}, bf16[2,4096,64]{1,2,0:T(8,128)(2,1)}, bf16[2,4096,64]{1,2,0:T(8,128)(2,1)}, bf16[2,4096,64]{...) while((s32[]{:T(128)}, f32[2,512,2,64]{1,3,2,0:T(8,128)S(1)}, ...), condition=%wide.region_36.37_spmd.clone, body=%wide.region_35.36_spmd.clone.sunk | while | flops 681247744 | bytes 23511300 | solution.py:427
  519.4 18.6 %fusion.69 = (f32[2,512,6]{1,2,0:T(8,128)}, f32[2,512,6]{1,2,0:T(8,128)}, f32[2,512,512]{2,1,0:T(8,128)S(1)}) fusion(f32[2,512,6]{1,2,0:T(8,128)S(1)} %bitcast.524, f32[2,512,512]{2,1,0:T(8,128)} %fusion.220, pred[2,512,512]{2,1,0:T(8,128)(4,1)} %compare_and_fusion.3, f32[2,512,6,64]{1,3,2,0:T(8,128)S(1)} %bitcast.508, f32[2,512,6]{1,2,0:T(8,128)S(1)} %copy-done.76, ...), kind=kOutput, calls=%fused_computation.88 | convolution fusion | flops 2450378752 | bytes 7962624 | tf_op jit(solution)/shard_map/transpose(jvp(rtsh,rshp->rthp))/dot_general | solution.py:122
  542.4 12.8 %fusion.64 = f32[2,6,64,512]{3,2,1,0:T(8,128)} fusion(f32[2,512,6]{1,2,0:T(8,128)S(1)} %bitcast.525, f32[2,512,512]{2,1,0:T(8,128)S(1)} %copy-done.50, pred[2,512,512]{2,1,0:T(8,128)(4,1)S(1)} %copy-done.79, f32[2,512,6,64]{1,3,2,0:T(8,128)S(1)} %copy-done.12), kind=kOutput, calls=%fused_computation.85 | convolution fusion | flops 2428502016 | bytes 5791744 | tf_op jit(solution)/shard_map/transpose(jvp(rtsh,rshp->rthp))/dot_general | solution.py:122
  557.5 22.7 %reduce-scatter.16.cloned.1.call-done = bf16[2,512,64]{1,2,0:T(8,128)(2,1)} async-done(((bf16[2,4096,64]{1,2,0:T(8,128)(2,1)}), bf16[2,512,64]{1,2,0:T(8,128)(2,1)}) %reduce-scatter.16.cloned.1.call-update) | async-done | bytes 131088 | tf_op jit(solution)/shard_map/reduce_scatter | solution.py:434
  584.7 23.1 %all-gather.24.cloned.1.call-done = bf16[16,6,64,128]{3,2,1,0:T(8,128)(2,1)} async-done(((bf16[2,6,64,128]{3,2,1,0:T(8,128)(2,1)}), bf16[16,6,64,128]{3,2,1,0:T(8,128)(2,1)}) %all-gather.24.cloned.1.call-update) | async-done | bytes 1572880 | tf_op jit(solution)/shard_map/all_gather | solution.py:29
  607.7 13.6 %while.85 = (s32[]{:T(128)}, f32[2,6,64,128]{3,2,1,0:T(8,128)S(1)}, s32[]{:T(128)}, bf16[8,2,6,64,128]{4,3,2,1,0:T(8,128)(2,1)}, bf16[8,2,6]{2,1,0:T(2,128)(2,1)...) while((s32[]{:T(128)}, f32[2,6,64,128]{3,2,1,0:T(8,128)S(1)}, s32[]{:T(128)}, ...), condition=%wide.region_20.21_spmd.clone, body=%wide.region_19.20_spmd.clone.sunk | while | flops 491540 | bytes 983335 | solution.py:47
  635.8 15.3 %reduce-window.26 = f32[2,6,4,128]{3,2,1,0:T(4,128)S(1)} reduce-window(f32[2,6,4,128]{3,2,1,0:T(4,128)S(1)} %reshape.789, f32[]{:T(128)} %constant.380.clone.1), window={size=1x1x1x128 pad=0_0x0_0x0_0x0_127}, to_apply=%region_32.33 | reduce-window | flops 780288 | bytes 49156 | tf_op jit(solution)/shard_map/reduce-window.4
  657.2 15.1 %reduce-window.24 = f32[2,6,4,128]{3,2,1,0:T(4,128)S(1)} reduce-window(f32[2,6,4,128]{3,2,1,0:T(4,128)S(1)} %reshape.788, f32[]{:T(128)} %constant.380.clone.1), window={size=1x1x1x128 pad=0_0x0_0x0_0x0_127}, to_apply=%region_27.28 | reduce-window | flops 780288 | bytes 49156 | tf_op jit(solution)/shard_map/reduce-window.2
  674.5 9.8 all-reduce.18.cloned.1.call-done
  690.1 14.6 %scatter-add.11 = f32[2,515,640]{1,2,0:T(8,128)} dynamic-update-slice(f32[2,515,640]{1,2,0:T(8,128)} %scatter-add.10, f32[2,512,640]{1,2,0:T(8,128)} %multiply_add_fusion, s32[]{:T(128)} %constant.377.clone.1, s32[]{:T(128)} %constant.384.clone.1, s32[]{:T(128)} %constant.377.clone.1) | dynamic-update-slice | bytes 5242884 | tf_op jit(solution)/shard_map/scatter-add | solution.py:494
  704.7 4.6 slice_add_fusion.1
  709.3 14.6 %scatter-add.14 = f32[2,515,640]{1,2,0:T(8,128)} dynamic-update-slice(f32[2,515,640]{1,2,0:T(8,128)} %scatter-add.11, f32[2,512,640]{1,2,0:T(8,128)} %slice_add_fusion.1, s32[]{:T(128)} %constant.377.clone.1, s32[]{:T(128)} %constant.383.clone.1, s32[]{:T(128)} %constant.377.clone.1) | dynamic-update-slice | bytes 5242884 | tf_op jit(solution)/shard_map/scatter-add | solution.py:494
  730.6 5.5 fusion.86
  738.3 4.4 multiply_reduce_fusion
  749.2 5.4 bitcast_convert_fusion.2
  772.6 14.3 %reduce-scatter.12.cloned.1.call-done = bf16[2,128,1024]{2,1,0:T(8,128)(2,1)} async-done(((bf16[2,512,1024]{2,1,0:T(8,128)(2,1)}), bf16[2,128,1024]{2,1,0:T(8,128)(2,1)}) %reduce-scatter.12.cloned.1.call-update) | async-done | bytes 524304 | tf_op jit(solution)/shard_map/reduce_scatter | solution.py:538
  793.5 41.0 %all-gather.12.cloned.1.call-done = bf16[2,512,1024]{2,1,0:T(8,128)(2,1)} async-done(((bf16[2,128,1024]{2,1,0:T(8,128)(2,1)}), bf16[2,512,1024]{2,1,0:T(8,128)(2,1)}) %all-gather.12.cloned.1.call-update) | async-done | bytes 2097168 | tf_op jit(solution)/shard_map/all_gather | solution.py:565
  835.2 118.5 %all-reduce.16.cloned.1.call-done = (bf16[1024,2,384]{2,0,1:T(8,128)(2,1)}, bf16[1024,2,128]{2,0,1:T(8,128)(2,1)}, bf16[1024,2,512]{2,0,1:T(8,128)(2,1)}, bf16[1...) async-done(((bf16[1024,2,384]{2,0,1:T(8,128)(2,1)}, ...) | async-done | bytes 7077904 | tf_op jit(solution)/shard_map/psum | solution.py:587
  971.8 19.5 %all-reduce.8 = (bf16[1,4,1024]{2,1,0:T(4,128)(2,1)S(1)}, bf16[1,4,1024]{2,1,0:T(4,128)(2,1)S(1)}) all-reduce(bf16[1,4,1024]{2,1,0:T(4,128)(2,1)S(1)} %broadcast_in_dim.378, bf16[1,4,1024]{2,1,0:T(4,128)(2,1)S(1)} %broadcast_in_dim.379), channel_id=11, replica_groups=mesh['seq'=8,'head'=4] {'head'}, use_global_device_ids=true, to_apply=%region_44.45.clone | all-reduce | flops 8192 | bytes 32768
  992.6 23.2 %all-reduce.6 = (bf16[1024]{0:T(1024)(128)(2,1)S(1)}, bf16[1024,6]{0,1:T(8,128)(2,1)S(1)}, bf16[6]{0:T(256)(128)(2,1)S(1)}, bf16[6]{0:T(256)(128)(2,1)S(1)}, bf1...) all-reduce(bf16[1024]{0:T(1024)(128)(2,1)S(1)} %dynamic-slice_reduc, ...), channel_id=1, replica_groups=mesh['seq'=8,'head'=4] {'seq'}, use_global_device_ids=true, to_apply=%region_45.46 | all-reduce | flops 10770 | bytes 43080 | tf_op jit(solution)/shard_map/psum | solution.py:586
  (748 shorter events, 408.5 us)
Async XLA Ops:
  7.2 313.9 %copy-start = (bf16[512,1024]{1,0:T(8,128)(2,1)S(1)}, bf16[512,1024]{1,0:T(8,128)(2,1)}, u32[]{:S(2)}) copy-start(bf16[512,1024]{1,0:T(8,128)(2,1)} %param.55) | copy-start | bytes 3145732
  7.2 87.1 %all-gather.22.cloned.1.call-start = ((), (), s32[]{:S(2)}) async-start(), calls=%async_computation.16 | async-start | bytes 1179648 | tf_op jit(solution)/shard_map/all_gather | solution.py:277
  9.6 55.1 %copy-start.94 = (f32[2,512]{1,0:T(2,128)}, f32[2,512]{1,0:T(2,128)S(1)}, u32[]{:S(2)}) copy-start(f32[2,512]{1,0:T(2,128)S(1)} %add_rsqrt_fusion.1) | copy-start | bytes 12292
  10.5 57.1 %copy-start.107 = (pred[2,512]{1,0:T(4,128)(4,1)}, pred[2,512]{1,0:T(4,128)(4,1)S(1)}, u32[]{:S(2)}) copy-start(pred[2,512]{1,0:T(4,128)(4,1)S(1)} %get-tuple-element.1263) | copy-start | bytes 3076
  10.5 25.7 %copy-start.92 = (f32[2,512]{1,0:T(2,128)}, f32[2,512]{1,0:T(2,128)S(1)}, u32[]{:S(2)}) copy-start(f32[2,512]{1,0:T(2,128)S(1)} %convert_element_type.385) | copy-start | bytes 12292
  17.3 118.4 %all-gather.20.cloned.1.call-start = ((), (), s32[]{:S(2)}) async-start(), calls=%async_computation.15 | async-start | bytes 1179648 | tf_op jit(solution)/shard_map/all_gather | solution.py:278
  29.2 52.4 %collective-permute-start = (bf16[2,3,640]{1,2,0:T(8,128)(2,1)}, bf16[2,3,640]{1,2,0:T(8,128)(2,1)}, u32[]{:S(2)}, u32[]{:S(2)}) collective-permute-start(bf16[2,3,640]{1,2,0:T(8,128)(2,1)} %fusion.192), channel_id=1, source_target_pairs={{0,4},{4,8},{8,12},{12,16},{16,20},{20,24},{24,28},{1,5},{5,9},{9,... | collective-permute-start | bytes 23048 | tf_op jit(solution)/shard_map/ppermute | solution.py:23
  34.0 154.6 %all-gather.18.cloned.1.call-start = ((), (), s32[]{:S(2)}) async-start(), calls=%async_computation.14 | async-start | bytes 1769472 | tf_op jit(solution)/shard_map/all_gather | solution.py:29
  38.1 28.7 %copy-start.59 = (f32[2,512,32]{1,2,0:T(8,128)}, f32[2,512,32]{1,2,0:T(8,128)S(1)}, u32[]{:S(2)}) copy-start(f32[2,512,32]{1,2,0:T(8,128)S(1)} %get-tuple-element.1248) | copy-start | bytes 393220
  44.3 22.4 %copy-start.103 = (u8[512,6]{0,1:T(8,128)(4,1)}, u8[512,6]{0,1:T(8,128)(4,1)S(1)}, u32[]{:S(2)}) copy-start(u8[512,6]{0,1:T(8,128)(4,1)S(1)} %fusion.250) | copy-start | bytes 9220
  94.3 218.5 %all-reduce.14.cloned.1.call-start = ((), (), s32[]{:S(2)}) async-start(), calls=%async_computation.5 | async-start | bytes 4194304 | tf_op jit(solution)/shard_map/psum | solution.py:335
  225.4 147.6 %reduce-scatter.10.cloned.1.call-start = ((), (), s32[]{:S(2)}) async-start(), calls=%async_computation.8 | async-start | bytes 2621440 | tf_op jit(solution)/shard_map/reduce_scatter | solution.py:364
  330.1 93.6 %all-gather.14.cloned.1.call-start = ((), (), s32[]{:S(2)}) async-start(), calls=%async_computation.9 | async-start | bytes 2621440 | tf_op jit(solution)/shard_map/all_gather | solution.py:371
  378.2 177.0 %reduce-scatter.14.cloned.1.call-start = ((), (), s32[]{:S(2)}) async-start(), calls=%async_computation.11 | async-start | bytes 1179648 | tf_op jit(solution)/shard_map/reduce_scatter | solution.py:431
  378.5 49.9 %copy-start.26 = (bf16[2,512,2,64]{1,3,2,0:T(8,128)(2,1)S(1)}, bf16[2,512,2,64]{1,3,2,0:T(8,128)(2,1)}, u32[]{:S(2)}) copy-start(bf16[2,512,2,64]{1,3,2,0:T(8,128)(2,1)} %get-tuple-element.1790) | copy-start | bytes 786436
  378.5 49.9 %copy-start.90 = (f32[2,2,512]{2,1,0:T(2,128)S(1)}, f32[2,2,512]{2,1,0:T(2,128)}, u32[]{:S(2)}) copy-start(f32[2,2,512]{2,1,0:T(2,128)} %get-tuple-element.1855) | copy-start | bytes 24580
  506.0 74.1 %reduce-scatter.16.cloned.1.call-start = ((), (), s32[]{:S(2)}) async-start(), calls=%async_computation.12 | async-start | bytes 1179648 | tf_op jit(solution)/shard_map/reduce_scatter | solution.py:434
  506.8 100.9 %all-gather.24.cloned.1.call-start = ((), (), s32[]{:S(2)}) async-start(), calls=%async_computation.17 | async-start | bytes 1769472 | tf_op jit(solution)/shard_map/all_gather | solution.py:29
  519.1 165.2 %all-reduce.18.cloned.1.call-start = ((), (), s32[]{:S(2)}) async-start(), calls=%async_computation.19 | async-start | bytes 2097152 | tf_op jit(solution)/shard_map/psum | solution.py:484
  519.4 23.0 %copy-start.50 = (f32[2,512,512]{2,1,0:T(8,128)S(1)}, f32[2,512,512]{2,1,0:T(8,128)}, u32[]{:S(2)}) copy-start(f32[2,512,512]{2,1,0:T(8,128)} %fusion.220) | copy-start | bytes 6291460
  631.8 111.0 %reduce-scatter.8.cloned.1.call-start = ((), (), s32[]{:S(2)}) async-start(), calls=%async_computation.6 | async-start | bytes 2621440 | tf_op jit(solution)/shard_map/reduce_scatter | solution.py:344
  635.0 151.9 %reduce-scatter.12.cloned.1.call-start = ((), (), s32[]{:S(2)}) async-start(), calls=%async_computation.10 | async-start | bytes 2621440 | tf_op jit(solution)/shard_map/reduce_scatter | solution.py:538
  655.0 49.7 %copy-start.3 = (f32[2,512,384]{1,2,0:T(8,128)}, f32[2,512,384]{1,2,0:T(8,128)S(1)}, u32[]{:S(2)}) copy-start(f32[2,512,384]{1,2,0:T(8,128)S(1)} %slice.306) | copy-start | bytes 4718596
  655.0 30.4 %copy-start.106 = (f32[640]{0:T(1024)S(1)}, f32[640]{0:T(1024)}, u32[]{:S(2)}) copy-start(f32[640]{0:T(1024)} %get-tuple-element.1098) | copy-start | bytes 7684
  655.2 30.3 %copy-start.113 = (pred[2,512]{1,0:T(4,128)(4,1)S(1)}, pred[2,512]{1,0:T(4,128)(4,1)}, u32[]{:S(2)}) copy-start(pred[2,512]{1,0:T(4,128)(4,1)} %get-tuple-element.1249) | copy-start | bytes 3076
  725.3 4.2 collective-permute-start.1
  742.7 91.7 %all-gather.12.cloned.1.call-start = ((), (), s32[]{:S(2)}) async-start(), calls=%async_computation.7 | async-start | bytes 2621440 | tf_op jit(solution)/shard_map/all_gather | solution.py:565
  745.3 208.4 %all-reduce.16.cloned.1.call-start = ((), (), s32[]{:S(2)}) async-start(), calls=%async_computation.18 | async-start | bytes 14155776 | tf_op jit(solution)/shard_map/psum | solution.py:587
  768.0 252.4 %all-gather.16.cloned.1.call-start = ((), (), s32[]{:S(2)}) async-start(), calls=%async_computation.13 | async-start | bytes 2621440 | tf_op jit(solution)/shard_map/all_gather | solution.py:566
  835.2 125.9 %copy-start.129 = (bf16[4,640]{1,0:T(4,128)(2,1)}, bf16[4,640]{1,0:T(4,128)(2,1)S(1)}, u32[]{:S(2)}) copy-start(bf16[4,640]{1,0:T(4,128)(2,1)S(1)} %maximum_convert_fusion) | copy-start | bytes 15364
  967.6 25.0 %slice-start = ((bf16[4,640]{1,0:T(4,128)(2,1)}), bf16[4,384]{1,0:T(4,128)(2,1)S(1)}, s32[]{:S(2)}) async-start(bf16[4,640]{1,0:T(4,128)(2,1)} %copy-done.129), calls=%async_computation.20 | async-start | bytes 6144 | tf_op jit(solution)/shard_map/slice | solution.py:593
  967.6 52.8 %copy-start.51 = (bf16[2,512,1024]{2,1,0:T(8,128)(2,1)S(1)}, bf16[2,512,1024]{2,1,0:T(8,128)(2,1)}, u32[]{:S(2)}) copy-start(bf16[2,512,1024]{2,1,0:T(8,128)(2,1)} %all-gather.12.cloned.1.call-done) | copy-start | bytes 6291460
  (147 other events, 615.7 us)
Sparse Core Ops, SparseCore 0:
  17.4 27.1 all-gather.21
  47.1 23.9 all-gather.19
  94.4 26.3 all-gather.17
  225.5 87.1 all-reduce.13
  330.2 42.7 reduce-scatter.9
  378.4 45.2 all-gather.13
  506.1 34.7 reduce-scatter.13
  544.1 36.0 reduce-scatter.15
  582.0 25.6 all-gather.23
  632.0 52.2 all-reduce.17
  687.3 43.1 reduce-scatter.7
  742.8 44.0 reduce-scatter.11
  789.2 45.2 all-gather.11
  840.8 112.9 all-reduce.15
  955.8 46.5 all-gather.15
where the time goes:
time: 1040 us; the launch traced here: 1030 us
  waiting for transfers between devices  403 us (39%)
  matrix products  255 us (25%)
  other arithmetic  173 us (17%)
  local copies, waits for them, and re-layouts  124 us (12%)
  blocking collectives  52.6 us (5%)
  between operations  16 us (2%)
    psum x1, waiting for transfers between devices, local(): lax.psum(mixer_proj_grad.astype(jnp.bfloat16), 'seq').astype(jnp.float32)  119 us
    psum x1, waiting for transfers between devices, local(): lax.psum((mixer_part + attend_part).astype(jnp.bfloat16), 'head')  86.9 us
    dot_general x3, matrix products, state_output(): jnp.einsum('rtsh,rshp->rthp', gram_mat[..., None] * decay_mat, drive_in,...  49.1 us
    all_gather x1, waiting for transfers between devices, local(): lax.all_gather(middle_grad_share.astype(jnp.bfloat16), 'head', axis=1, ti...  45.2 us
    another operation x12, other arithmetic  41.9 us
    reduce_scatter x1, waiting for transfers between devices, local(): lax.psum_scatter(middle_low_part.astype(jnp.bfloat16), 'head', scatter_di...  41.6 us
    all_gather x1, waiting for transfers between devices, local(): lax.all_gather(output_share, 'head', axis=1, tiled=True)  41 us
    unnamed x299, local copies, waits for them, and re-layouts  39.8 us
  transfers between devices with their start and end apart: 17, of which 9 were waited for; matrix products, arithmetic and copies ran while one was open for 35% of the time, Pallas kernels for 0%

commit v1 on v0

--- a/solution.py
+++ b/solution.py
@@ -4,6 +4,8 @@
 import jax
 import jax.numpy as jnp
 from jax import lax
+from jax.experimental import pallas as pl
+from jax.experimental.pallas import tpu as pltpu
 from jax.sharding import PartitionSpec as P
 
 ATT_HEADS = 8
@@ -12,9 +14,10 @@
 
 
 EPSILON = 1e-05
-PRECISE = lax.Precision.HIGHEST
+PRECISE = lax.Precision.DEFAULT
 ROPE_BASE = 10000.0
 FLOOR_SCORE = -1e30
+FIRST_TOP = -1e29
 
 
 def shifted(block, axis, distance):
@@ -23,28 +26,28 @@
     return lax.ppermute(block, axis, route)
 
 
-def carried_in(shard, axis, combine, identity, reverse):
-    size, index = (lax.axis_size(axis), lax.axis_index(axis))
-    everything = jax.tree.map(
-        lambda part, kind: lax.all_gather(part.astype(kind), axis),
-        shard,
-        (jnp.bfloat16, jnp.bfloat16),
-    )
-    start = jax.tree.map(
-        lambda part, zero: jnp.broadcast_to(jnp.asarray(zero, part.dtype), part.shape),
-        shard,
-        identity,
-    )
-
-    def turn(k, before):
-        at = size - 1 - k if reverse else k
-        reached = at > index if reverse else at < index
-        new = combine(
-            before, jax.tree.map(lambda part, own: part[at].astype(own.dtype), everything, shard)
-        )
-        return jax.tree.map(lambda a, b: jnp.where(reached, a, b), new, before)
-
-    return lax.fori_loop(0, size, turn, start)
+def carried_in(keeps, states, index, reverse):
+    size = keeps.shape[0]
+    order = jnp.arange(size)
+    source, between = order[:, None], order[None, :]
+    if reverse:
+        inside = (between < source) & (between > index)
+        reached = order > index
+    else:
+        inside = (between > source) & (between < index)
+        reached = order < index
+    weight = jnp.prod(
+        jnp.where(inside[:, :, None, None], keeps.astype(jnp.float32)[None], 1.0), axis=1
+    )
+    weight = jnp.where(reached[:, None, None], weight, 0.0)
+    return jnp.sum(weight[..., None, None] * states.astype(jnp.float32), axis=0)
+
+
+def running_sum(values):
+    length = values.shape[1]
+    steps = jnp.arange(length)
+    lower = (steps[:, None] >= steps[None, :]).astype(jnp.float32)
+    return jnp.einsum("ts,rsh->rth", lower, values, precision=lax.Precision.HIGHEST)
 
 
 def silu_value(values):
@@ -96,7 +99,7 @@
 
 def state_summary(doc_ids, positions, inner_act, b_vec, step_size, log_keep):
     piece_len = inner_act.shape[1]
-    cum_keep = jnp.cumsum(log_keep, axis=1)
+    cum_keep = running_sum(log_keep)
     drive_in = inner_act * step_size[..., None]
     tail_rate = jnp.where(
         (doc_ids == doc_ids[:, -1:])[:, :, None], jnp.exp(cum_keep[:, -1:, :] - cum_keep), 0.0
@@ -109,7 +112,7 @@
 def state_output(doc_ids, positions, inner_act, b_vec, c_vec, step_size, log_keep, entering):
     piece_len = inner_act.shape[1]
     local_place = jnp.arange(piece_len, dtype=jnp.int32)
-    cum_keep = jnp.cumsum(log_keep, axis=1)
+    cum_keep = running_sum(log_keep)
     causal_mask = (local_place[:, None] >= local_place[None, :])[None] & (
         doc_ids[:, :, None] == doc_ids[:, None, :]
     )
@@ -129,31 +132,135 @@
     )
 
 
-def carry_forward(earlier, later):
-    keep_early, state_early = earlier
-    keep_late, state_late = later
-    return (keep_early * keep_late, keep_late[..., None, None] * state_early + state_late)
-
-
-def carry_backward(earlier, later):
-    keep_early, grad_early = earlier
-    keep_late, grad_late = later
-    return (keep_late * keep_early, grad_late + keep_late[..., None, None] * grad_early)
-
-
-def score_block(queries, key_piece, key_places, key_docs, query_places, query_docs, score_scale):
-    raw_scores = (
-        jnp.einsum("rthd,rsd->rhts", queries, key_piece, preferred_element_type=jnp.float32)
-        * score_scale
-    )
-    allowed = (key_places[None, None, :] <= query_places[:, :, None]) & (
-        key_docs[:, None, :] == query_docs[:, :, None]
-    )
-    return (raw_scores, allowed[:, None])
-
-
-def block_probs(raw_scores, allowed, row_top, row_total):
-    return jnp.where(allowed, jnp.exp(raw_scores - row_top[..., None]) / row_total[..., None], 0.0)
+def inner_dot(left, right):
+    return lax.dot_general(left, right, (((1,), (1,)), ((), ())), preferred_element_type=jnp.float32)
+
+
+def attend_kernel(span, low_ref, high_ref, query_ref, place_ref, begin_ref, kv_ref, kvt_ref, out_ref, stat_ref):
+    row = pl.program_id(0)
+    dim = query_ref.shape[2]
+    width = query_ref.shape[1]
+    query = query_ref[0]
+    place = place_ref[0]
+    begin = begin_ref[0]
+
+    def step(block, carry):
+        top, total, acc = carry
+        at = pl.multiple_of(block * span, span)
+        key = kv_ref[0, pl.ds(at, span), :dim]
+        value_t = kvt_ref[0, dim:, pl.ds(at, span)]
+        scores = inner_dot(key, query)
+        key_place = at + lax.broadcasted_iota(jnp.int32, scores.shape, 0)
+        allowed = (key_place <= place) & (key_place >= begin)
+        scores = jnp.where(allowed, scores, FLOOR_SCORE)
+        new_top = jnp.maximum(top, jnp.max(scores, axis=0, keepdims=True))
+        probs = jnp.exp(scores - new_top)
+        scale = jnp.exp(top - new_top)
+        total = total * scale + jnp.sum(probs, axis=0, keepdims=True)
+        acc = acc * scale + jnp.dot(
+            value_t, probs.astype(jnp.bfloat16), preferred_element_type=jnp.float32
+        )
+        return new_top, total, acc
+
+    top, total, acc = lax.fori_loop(
+        low_ref[row],
+        high_ref[row],
+        step,
+        (
+            jnp.full((1, width), FIRST_TOP, jnp.float32),
+            jnp.zeros((1, width), jnp.float32),
+            jnp.zeros((dim, width), jnp.float32),
+        ),
+    )
+    out_ref[0] = acc / total
+    stat_ref[0] = top + jnp.log(total)
+
+
+def attend_back_kernel(
+    span, low_ref, high_ref, query_ref, grad_ref, place_ref, begin_ref, stat_ref, dot_ref, kv_ref, kvt_ref,
+    query_grad_ref, kv_grad_ref,
+):
+    row = pl.program_id(0)
+    dim = query_ref.shape[2]
+    width = query_ref.shape[1]
+    query = query_ref[0]
+    grad = grad_ref[0]
+    place = place_ref[0]
+    begin = begin_ref[0]
+    stat = stat_ref[0]
+    dots = dot_ref[0]
+    kv_grad_ref[...] = jnp.zeros_like(kv_grad_ref)
+
+    def step(block, query_grad):
+        at = pl.multiple_of(block * span, span)
+        key = kv_ref[0, pl.ds(at, span), :dim]
+        value = kv_ref[0, pl.ds(at, span), dim:]
+        key_t = kvt_ref[0, :dim, pl.ds(at, span)]
+        scores = inner_dot(key, query)
+        key_place = at + lax.broadcasted_iota(jnp.int32, scores.shape, 0)
+        allowed = (key_place <= place) & (key_place >= begin)
+        probs = jnp.exp(jnp.where(allowed, scores - stat, FLOOR_SCORE))
+        prob_grad = inner_dot(value, grad)
+        score_grad = (probs * (prob_grad - dots)).astype(jnp.bfloat16)
+        value_grad = jnp.dot(probs.astype(jnp.bfloat16), grad, preferred_element_type=jnp.float32)
+        key_grad = jnp.dot(score_grad, query, preferred_element_type=jnp.float32)
+        kv_grad_ref[0, pl.ds(at, span), :] = jnp.concatenate(
+            [key_grad, value_grad], axis=1
+        ).astype(jnp.bfloat16)
+        return query_grad + jnp.dot(key_t, score_grad, preferred_element_type=jnp.float32)
+
+    query_grad_ref[0] = lax.fori_loop(
+        low_ref[row], high_ref[row], step, jnp.zeros((dim, width), jnp.float32)
+    )
+
+
+def row_spec(*shape):
+    return pl.BlockSpec((1,) + shape, lambda r, *_: (r,) + (0,) * len(shape))
+
+
+def attend_forward(span, low, high, query, place, begin, keyval, keyval_t):
+    rows, width, dim = query.shape
+    full = keyval.shape[1]
+    return pl.pallas_call(
+        partial(attend_kernel, span),
+        grid_spec=pltpu.PrefetchScalarGridSpec(
+            num_scalar_prefetch=2,
+            grid=(rows,),
+            in_specs=[
+                row_spec(width, dim), row_spec(1, width), row_spec(1, width),
+                row_spec(full, 2 * dim), row_spec(2 * dim, full),
+            ],
+            out_specs=[row_spec(dim, width), row_spec(1, width)],
+        ),
+        out_shape=[
+            jax.ShapeDtypeStruct((rows, dim, width), jnp.float32),
+            jax.ShapeDtypeStruct((rows, 1, width), jnp.float32),
+        ],
+        compiler_params=pltpu.CompilerParams(vmem_limit_bytes=48 * 1024 * 1024),
+    )(low, high, query, place, begin, keyval, keyval_t)
+
+
+def attend_backward(span, low, high, query, grad, place, begin, stat, dots, keyval, keyval_t):
+    rows, width, dim = query.shape
+    full = keyval.shape[1]
+    return pl.pallas_call(
+        partial(attend_back_kernel, span),
+        grid_spec=pltpu.PrefetchScalarGridSpec(
+            num_scalar_prefetch=2,
+            grid=(rows,),
+            in_specs=[
+                row_spec(width, dim), row_spec(width, dim), row_spec(1, width), row_spec(1, width),
+                row_spec(1, width), row_spec(1, width),
+                row_spec(full, 2 * dim), row_spec(2 * dim, full),
+            ],
+            out_specs=[row_spec(dim, width), row_spec(full, 2 * dim)],
+        ),
+        out_shape=[
+            jax.ShapeDtypeStruct((rows, dim, width), jnp.float32),
+            jax.ShapeDtypeStruct((rows, full, 2 * dim), jnp.bfloat16),
+        ],
+        compiler_params=pltpu.CompilerParams(vmem_limit_bytes=48 * 1024 * 1024),
+    )(low, high, query, grad, place, begin, stat, dots, keyval, keyval_t)
 
 
 def local(
@@ -178,7 +285,6 @@
     ffn_down,
 ):
     row_count, length, model_width = tokens.shape
-    seq_count = lax.axis_size("seq")
     offset = lax.axis_index("seq") * length
     head_ways = lax.axis_size("head")
     share_len = length // head_ways
@@ -243,12 +349,10 @@
     (fresh_state, keep_rate), summary_back = jax.vjp(
         partial(state_summary, doc_ids, positions), mixer_act, state_b, step_size, log_keep
     )
-    chain_keep, entering = carried_in(
-        (keep_rate, fresh_state),
-        "seq",
-        carry_forward,
-        (jnp.ones_like(keep_rate), jnp.zeros_like(fresh_state)),
-        False,
+    seq_index = lax.axis_index("seq")
+    all_keep = lax.all_gather(keep_rate.astype(jnp.bfloat16), "seq")
+    entering = carried_in(
+        all_keep, lax.all_gather(fresh_state.astype(jnp.bfloat16), "seq"), seq_index, False
     )
     mixed_state, output_back = jax.vjp(
         partial(state_output, doc_ids, positions),
@@ -273,61 +377,24 @@
     ).astype(jnp.bfloat16)
     key_rot = rotate(keyval_pre[:, :, 0][:, :, None], positions, 1.0)[:, :, 0].astype(jnp.bfloat16)
     value_low = keyval_pre[:, :, 1].astype(jnp.bfloat16)
-    all_keys, all_values = (
-        lax.all_gather(key_rot, "seq", axis=1, tiled=True),
-        lax.all_gather(value_low, "seq", axis=1, tiled=True),
-    )
-    full_len = all_keys.shape[1]
-    key_docs = doc_layout(doc_starts, 0, full_len)[0]
-    per_block = math.gcd(seq_count, max(1, 512 // length))
-    block_span = length * per_block
-    block_total = full_len // block_span
-    query_places = (offset + places)[None, :]
-
-    def key_piece_at(block_start):
-        key_piece = lax.dynamic_slice_in_dim(all_keys, block_start, block_span, 1)
-        value_piece = lax.dynamic_slice_in_dim(all_values, block_start, block_span, 1)
-        doc_piece = lax.dynamic_slice_in_dim(key_docs, block_start, block_span, 1)
-        key_places = block_start + jnp.arange(block_span, dtype=jnp.int32)
-        return (key_piece, value_piece, doc_piece, key_places)
-
-    def stats_step(block_index, loop_carry):
-        row_top, row_total = loop_carry
-        key_piece, value_piece, doc_piece, key_places = key_piece_at(block_index * block_span)
-        raw_scores, allowed = score_block(
-            query_rot, key_piece, key_places, doc_piece, query_places, doc_ids, score_scale
-        )
-        masked = jnp.where(allowed, raw_scores, FLOOR_SCORE)
-        new_top = jnp.maximum(row_top, jnp.max(masked, axis=-1))
-        row_total = row_total * jnp.exp(row_top - new_top) + jnp.sum(
-            jnp.where(allowed, jnp.exp(masked - new_top[..., None]), 0.0), axis=-1
-        )
-        return (new_top, row_total)
-
-    stat_shape = (row_count, local_heads, length)
-    row_top, row_total = lax.fori_loop(
-        0,
-        block_total,
-        stats_step,
-        (jnp.full(stat_shape, FLOOR_SCORE, jnp.float32), jnp.zeros(stat_shape, jnp.float32)),
-    )
-
-    def value_step(block_index, attend_acc):
-        key_piece, value_piece, doc_piece, key_places = key_piece_at(block_index * block_span)
-        raw_scores, allowed = score_block(
-            query_rot, key_piece, key_places, doc_piece, query_places, doc_ids, score_scale
-        )
-        probs_low = block_probs(raw_scores, allowed, row_top, row_total).astype(jnp.bfloat16)
-        return attend_acc + jnp.einsum(
-            "rhts,rsd->rthd", probs_low, value_piece, preferred_element_type=jnp.float32
-        )
-
-    attended = lax.fori_loop(
-        0,
-        block_total,
-        value_step,
-        jnp.zeros((row_count, length, local_heads, ATT_DIM), jnp.float32),
-    )
+    keyval_all = lax.all_gather(
+        jnp.concatenate([key_rot, value_low], axis=2), "seq", axis=1, tiled=True
+    )
+    keyval_t = jnp.swapaxes(keyval_all, 1, 2)
+    query_scaled = (
+        jnp.swapaxes(query_rot, 1, 2).reshape(row_count, local_heads * length, ATT_DIM)
+        * jnp.bfloat16(score_scale)
+    )
+    begins = offset + places[None, :] - positions
+    place_row = jnp.tile(offset + places, local_heads)[None, None, :]
+    place_row = jnp.broadcast_to(place_row, (row_count, 1, local_heads * length))
+    begin_row = jnp.tile(begins, (1, local_heads))[:, None, :]
+    low_block = begins[:, 0] // length
+    high_block = jnp.broadcast_to(lax.axis_index("seq") + 1, (row_count,)).astype(jnp.int32)
+    attended_t, stat_row = attend_forward(
+        length, low_block, high_block, query_scaled, place_row, begin_row, keyval_all, keyval_t
+    )
+    attended = attended_t.reshape(row_count, ATT_DIM, local_heads, length).transpose(0, 3, 2, 1)
     attended_low = attended.astype(jnp.bfloat16).reshape(row_count, length, local_heads * ATT_DIM)
     attend_part = jnp.einsum(
         "rtc,cd->rtd", attended_low, attend_down, preferred_element_type=jnp.float32
@@ -384,57 +451,27 @@
     attended_grad = attended_grad.reshape(row_count, length, local_heads, ATT_DIM)
     grad_dot = jnp.swapaxes(jnp.sum(attended_grad.astype(jnp.float32) * attended, axis=-1), 1, 2)
 
-    def query_side(block_start):
-        key_piece, value_piece, doc_piece, key_places = key_piece_at(block_start)
-        raw_scores, allowed = score_block(
-            query_rot, key_piece, key_places, doc_piece, query_places, doc_ids, score_scale
-        )
-        soft_probs = block_probs(raw_scores, allowed, row_top, row_total)
-        prob_grad = jnp.einsum(
-            "rthd,rsd->rhts", attended_grad, value_piece, preferred_element_type=jnp.float32
-        )
-        score_grad = (soft_probs * (prob_grad - grad_dot[..., None])).astype(jnp.bfloat16)
-        return (soft_probs, score_grad, key_piece)
-
-    query_zero = jnp.zeros((row_count, length, local_heads, ATT_DIM), jnp.float32)
-
-    def reduce_step(block_index, loop_carry):
-        query_grad, key_grads, value_grads = loop_carry
-        block_start = block_index * block_span
-        soft_probs, score_grad, key_piece = query_side(block_start)
-        query_grad = (
-            query_grad
-            + jnp.einsum(
-                "rhts,rsd->rthd", score_grad, key_piece, preferred_element_type=jnp.float32
-            )
-            * score_scale
-        )
-        key_block = (
-            jnp.einsum("rhts,rthd->rsd", score_grad, query_rot, preferred_element_type=jnp.float32)
-            * score_scale
-        )
-        value_block = jnp.einsum(
-            "rhts,rthd->rsd",
-            soft_probs.astype(jnp.bfloat16),
-            attended_grad,
-            preferred_element_type=jnp.float32,
-        )
-        key_grads = lax.dynamic_update_slice_in_dim(key_grads, key_block, block_start, 1)
-        value_grads = lax.dynamic_update_slice_in_dim(value_grads, value_block, block_start, 1)
-        return (query_grad, key_grads, value_grads)
-
-    full_zero = jnp.zeros((row_count, full_len, ATT_DIM), jnp.float32)
-    query_grad, key_grads, value_grads = lax.fori_loop(
-        0, block_total, reduce_step, (query_zero, full_zero, full_zero)
-    )
-    key_grad, value_grad = (
-        lax.psum_scatter(
-            key_grads.astype(jnp.bfloat16), "seq", scatter_dimension=1, tiled=True
-        ).astype(jnp.float32),
-        lax.psum_scatter(
-            value_grads.astype(jnp.bfloat16), "seq", scatter_dimension=1, tiled=True
-        ).astype(jnp.float32),
-    )
+    query_grad_t, keyval_grads = attend_backward(
+        length,
+        low_block,
+        high_block,
+        query_scaled,
+        jnp.swapaxes(attended_grad, 1, 2).reshape(row_count, local_heads * length, ATT_DIM),
+        place_row,
+        begin_row,
+        stat_row,
+        grad_dot.reshape(row_count, 1, local_heads * length),
+        keyval_all,
+        keyval_t,
+    )
+    query_grad = (
+        query_grad_t.reshape(row_count, ATT_DIM, local_heads, length).transpose(0, 3, 2, 1)
+        * score_scale
+    )
+    keyval_grad = lax.psum_scatter(
+        keyval_grads, "seq", scatter_dimension=1, tiled=True
+    ).astype(jnp.float32)
+    key_grad, value_grad = keyval_grad[..., :ATT_DIM], keyval_grad[..., ATT_DIM:]
     query_low = (
         rotate(query_grad, positions, -1.0)
         .reshape(row_count, length, local_heads * ATT_DIM)
@@ -451,17 +488,13 @@
     gate_grad = gated_grad * full_state * silu_slope(gate_view)
     skip_gain_grad = jnp.sum(state_grad * mixer_act, axis=(0, 1, 3))
     lift_rate = jnp.where(
-        (positions > places)[:, :, None], jnp.exp(jnp.cumsum(log_keep, axis=1)), 0.0
+        (positions > places)[:, :, None], jnp.exp(running_sum(log_keep)), 0.0
     )
     local_grad = jnp.einsum(
         "rthp,rtn->rhpn", state_grad * lift_rate[..., None], state_c, precision=PRECISE
     )
-    chain_back, after_grad = carried_in(
-        (keep_rate, local_grad),
-        "seq",
-        carry_backward,
-        (jnp.ones_like(keep_rate), jnp.zeros_like(local_grad)),
-        True,
+    after_grad = carried_in(
+        all_keep, lax.all_gather(local_grad.astype(jnp.bfloat16), "seq"), seq_index, True
     )
     keep_grad = jnp.sum(after_grad * entering, axis=(2, 3))
     act_grad_one, b_grad_one, step_grad_one, log_grad_one = summary_back((after_grad, keep_grad))
@@ -491,8 +524,8 @@
         lag_steps = tap_count - 1 - tap_index
         masked = jnp.where((positions >= lag_steps)[:, :, None], pre_grad, 0.0)
         conv_grads.append(jnp.sum(masked * padded[:, tap_index : tap_index + length], axis=(0, 1)))
-        padded_grad = padded_grad.at[:, tap_index : tap_index + length].add(
-            masked * conv_weight[tap_index]
+        padded_grad = padded_grad + jnp.pad(
+            masked * conv_weight[tap_index], ((0, 0), (tap_index, lag_steps), (0, 0))
         )
     conv_weight_grad = jnp.stack(conv_grads, axis=0)
     rim_grad = shifted(padded_grad[:, : tap_count - 1], "seq", -1)

time: 1040 us -> 802 us (0.77)
  matrix products: 255 us -> 106 us
  other arithmetic: 173 us -> 65.1 us
  waiting for transfers between devices: 403 us -> 465 us
  local copies, waits for them, and re-layouts: 124 us -> 70.2 us
    dot_general x56 -> x3, matrix products: 113 us -> 1.25 us  [running_sum(): jnp.einsum('ts,rsh->rth', lower, values, precision=lax.Precision.HIGHEST)]
    another operation x12 -> x5, other arithmetic: 41.9 us -> 3.72 us
    psum x1, waiting for transfers between devices: 9.81 us -> 41.3 us  [local(): lax.psum(pre_grad[:, :, inner_width:].astype(jnp.bfloat16), 'head')]
    scatter-add x3 -> x0, local copies, waits for them, and re-layouts: 31.1 us -> none  [local(): padded_grad.at[:, tap_index:tap_index + length]]
    dot_general x3, matrix products: 49.1 us -> 22.8 us  [state_output(): jnp.einsum('rtsh,rshp->rthp', gram_mat[..., None] * decay_mat, drive_in,...]
    and x24 -> x2, other arithmetic: 17 us -> 0.02 us  [the longest x1 0.01 us: carried_in(): inside = (between < source) & (between > index)]
    select_n x16 -> x3, other arithmetic: 16.8 us -> 0.02 us  [the longest x2 0.01 us: carried_in(): weight = jnp.where(reached[:, None, None], weight, 0.0)]
    dynamic_slice x24 -> x0, local copies, waits for them, and re-layouts: 16.5 us -> none  [key_piece_at(): doc_piece = lax.dynamic_slice_in_dim(key_docs, block_start, block_span, 1)]
  transfers between devices with their start and end apart: 17 -> 15, of which waited for: 9 -> 11; matrix products, arithmetic and copies ran while one was open for 35% -> 20% of each run, Pallas kernels for 0% -> 1%
where the time goes in v1:
time: 802 us; the launch traced here: 793 us
  waiting for transfers between devices  465 us (58%)
  matrix products  106 us (13%)
  local copies, waits for them, and re-layouts  70.2 us (9%)
  other arithmetic  65.1 us (8%)
  blocking collectives  56.3 us (7%)
  between operations  16.4 us (2%)
  Pallas kernels  8.74 us (1%)
    psum x1, waiting for transfers between devices, local(): lax.psum(mixer_proj_grad.astype(jnp.bfloat16), 'seq').astype(jnp.float32)  118 us
    psum x1, waiting for transfers between devices, local(): lax.psum((mixer_part + attend_part).astype(jnp.bfloat16), 'head')  97.4 us
    unnamed x341, local copies, waits for them, and re-layouts  46.3 us
    all_gather x1, waiting for transfers between devices, local(): lax.all_gather(middle_grad_share.astype(jnp.bfloat16), 'head', axis=1, ti...  45.4 us
    reduce_scatter x1, waiting for transfers between devices, local(): lax.psum_scatter(middle_low_part.astype(jnp.bfloat16), 'head', scatter_di...  42.9 us
    psum x1, waiting for transfers between devices, local(): lax.psum(pre_grad[:, :, inner_width:].astype(jnp.bfloat16), 'head')  41.3 us
    all_gather x1, waiting for transfers between devices, local(): lax.all_gather(output_share, 'head', axis=1, tiled=True)  40.9 us
    reduce_scatter x1, waiting for transfers between devices, local(): lax.psum_scatter(keyval_grads, 'seq', scatter_dimension=1, tiled=True)  25 us
  transfers between devices with their start and end apart: 15, of which 11 were waited for; matrix products, arithmetic and copies ran while one was open for 20% of the time, Pallas kernels for 1%

profile of v1, /device:TPU:0, one launch (start us, length us, event | category | flops | bytes accessed | tf_op | source)
XLA Modules:
  0.0 793.0 jit_solution(316804665934050047)
XLA Ops:
  9.4 5.0 copy.364
  14.5 3.4 fusion.42
  28.7 4.5 multiply_convert_fusion.2
  49.3 13.7 %all_gather.28 = bf16[8,2,6]{2,1,0:T(2,128)(2,1)S(1)} all-gather(bf16[1,2,6]{2,1,0:T(2,128)(2,1)S(1)} %fusion.215), channel_id=1, replica_groups=mesh['seq'=8,'head'=4] {'seq'}, dimensions={0}, use_global_device_ids=true | all-gather | bytes 216 | tf_op jit(solution)/shard_map/all_gather | solution.py:353
  70.7 7.4 multiply_convert_fusion.7
  78.1 19.4 %all-gather.9.cloned.1.call-done = bf16[2,4096,128]{1,2,0:T(8,128)(2,1)} async-done(((bf16[2,512,128]{1,2,0:T(8,128)(2,1)}), bf16[2,4096,128]{1,2,0:T(8,128)(2,1)}) %all-gather.9.cloned.1.call-update) | async-done | bytes 2097168 | tf_op jit(solution)/shard_map/all_gather | solution.py:380
  97.5 4.2 copy.381.kv_ref
  112.0 97.4 %all-reduce.17.cloned.1.call-done = bf16[2,512,1024]{2,1,0:T(8,128)(2,1)} async-done(((bf16[2,512,1024]{2,1,0:T(8,128)(2,1)}), bf16[2,512,1024]{2,1,0:T(8,128)(2,1)}) %all-reduce.17.cloned.1.call-update) | async-done | bytes 2097168 | tf_op jit(solution)/shard_map/psum | solution.py:402
  209.4 4.4 convert_add_fusion
  221.6 3.7 bitcast_convert_fusion.1
  225.4 42.9 %reduce-scatter.9.cloned.1.call-done = bf16[2,128,1024]{2,1,0:T(8,128)(2,1)} async-done(((bf16[2,512,1024]{2,1,0:T(8,128)(2,1)}), bf16[2,128,1024]{2,1,0:T(8,128)(2,1)}) %reduce-scatter.9.cloned.1.call-update) | async-done | bytes 524304 | tf_op jit(solution)/shard_map/reduce_scatter | solution.py:431
  273.2 45.4 %all-gather.13.cloned.1.call-done = bf16[2,512,1024]{2,1,0:T(8,128)(2,1)} async-done(((bf16[2,128,1024]{2,1,0:T(8,128)(2,1)}), bf16[2,512,1024]{2,1,0:T(8,128)(2,1)}) %all-gather.13.cloned.1.call-update) | async-done | bytes 2097168 | tf_op jit(solution)/shard_map/all_gather | solution.py:438
  318.6 4.1 fusion.70
  328.3 3.3 fusion.138
  335.6 5.7 shard_map.323
  343.4 4.3 copy.401
  349.2 10.1 %fusion.11 = (f32[2,512,6]{1,2,0:T(8,128)}, f32[2,512,6]{1,2,0:T(8,128)}, bf16[2,512,512]{2,1,0:T(8,128)(2,1)S(1)}) fusion(f32[2,512,6]{1,2,0:T(8,128)S(1)} %bitcast.424, f32[2,512,512]{2,1,0:T(8,128)} %fusion.172, pred[2,512,512]{2,1,0:T(8,128)(4,1)} %copy-done.88, f32[2,512,6,64]{1,3,2,0:T(8,128)S(1)} %bitcast.399, f32[2,512,6]{1,2,0:T(8,128)S(1)} %add_select_fusion, ...), kind=kOutput, calls=%fused_computation.12 | convolution fusion | flops 437112832 | bytes 6914048 | tf_op jit(solution)/shard_map/transpose(jvp(rtsh,rshp->rthp))/dot_general | solution.py:125
  362.5 5.2 fusion.6
  378.4 25.0 %reduce-scatter.13.cloned.1.call-done = bf16[2,512,128]{1,2,0:T(8,128)(2,1)} async-done(((bf16[2,4096,128]{1,2,0:T(8,128)(2,1)}), bf16[2,512,128]{1,2,0:T(8,128)(2,1)}) %reduce-scatter.13.cloned.1.call-update) | async-done | bytes 262160 | tf_op jit(solution)/shard_map/reduce_scatter | solution.py:471
  418.0 41.3 %all-reduce.21.cloned.1.call-done = (bf16[2,512,256]{1,2,0:T(8,128)(2,1)}, bf16[2,512,2,128]{3,1,2,0:T(8,128)(2,1)}) async-done(((bf16[2,512,256]{1,2,0:T(8,128)(2,1)}, bf16[2,512,2,128]{3,1,2,0:T(8,128)(2,1)}), (bf16[2,512,256]{1,2,0:T(8,128)(2,1)}, bf16[2,512,2,128]{3,1,2,0:T(8,128)(2,1)})) %all-reduce.21.cloned.1.call-update) | async-done | bytes 1048592 | tf_op jit(solution)/shard_map/psum | solution.py:517
  469.9 8.3 %pad_add_fusion = f32[2,515,640]{1,2,0:T(8,128)} fusion(f32[2,512,640]{1,2,0:T(8,128)} %copy-done.25, f32[2,512,640]{1,2,0:T(8,128)} %copy-done.24, f32[2,512,640]{1,2,0:T(8,128)} %copy-done.26, f32[2,512,640]{1,2,0:T(8,128)} %copy-done.23), kind=kLoop, calls=%fused_computation.36 | loop fusion | flops 1977600 | bytes 13122560 | tf_op jit(solution)/shard_map/add | solution.py:527
  483.4 6.9 multiply_reduce_fusion
  490.3 15.0 %reduce-scatter.7.cloned.1.call-done = bf16[2,128,1024]{2,1,0:T(8,128)(2,1)} async-done(((bf16[2,512,1024]{2,1,0:T(8,128)(2,1)}), bf16[2,128,1024]{2,1,0:T(8,128)(2,1)}) %reduce-scatter.7.cloned.1.call-update) | async-done | bytes 524304 | tf_op jit(solution)/shard_map/reduce_scatter | solution.py:411
  508.0 4.3 bitcast_convert_fusion.3
  512.3 5.7 bitcast_convert_fusion
  533.0 18.5 %reduce-scatter.11.cloned.1.call-done = bf16[2,128,1024]{2,1,0:T(8,128)(2,1)} async-done(((bf16[2,512,1024]{2,1,0:T(8,128)(2,1)}), bf16[2,128,1024]{2,1,0:T(8,128)(2,1)}) %reduce-scatter.11.cloned.1.call-update) | async-done | bytes 524304 | tf_op jit(solution)/shard_map/reduce_scatter | solution.py:571
  558.0 40.9 %all-gather.11.cloned.1.call-done = bf16[2,512,1024]{2,1,0:T(8,128)(2,1)} async-done(((bf16[2,128,1024]{2,1,0:T(8,128)(2,1)}), bf16[2,512,1024]{2,1,0:T(8,128)(2,1)}) %all-gather.11.cloned.1.call-update) | async-done | bytes 2097168 | tf_op jit(solution)/shard_map/all_gather | solution.py:598
  599.7 117.9 %all-reduce.19.cloned.1.call-done = (bf16[1024,2,384]{2,0,1:T(8,128)(2,1)}, bf16[1024,2,128]{2,0,1:T(8,128)(2,1)}, bf16[1024,2,512]{2,0,1:T(8,128)(2,1)}, bf16[1...) async-done(((bf16[1024,2,384]{2,0,1:T(8,128)(2,1)}, ...) | async-done | bytes 7077904 | tf_op jit(solution)/shard_map/psum | solution.py:620
  717.6 4.8 copy.415
  728.0 4.2 copy.417
  733.8 19.5 %all-reduce.11 = (bf16[1,4,1024]{2,1,0:T(4,128)(2,1)S(1)}, bf16[1,4,1024]{2,1,0:T(4,128)(2,1)S(1)}) all-reduce(bf16[1,4,1024]{2,1,0:T(4,128)(2,1)S(1)} %broadcast_in_dim.305, bf16[1,4,1024]{2,1,0:T(4,128)(2,1)S(1)} %broadcast_in_dim.306), channel_id=8, replica_groups=mesh['seq'=8,'head'=4] {'head'}, use_global_device_ids=true, to_apply=%region_28.29.clone | all-reduce | flops 8192 | bytes 32768
  754.6 23.2 %all-reduce.9 = (bf16[1024]{0:T(1024)(128)(2,1)S(1)}, bf16[1024,6]{0,1:T(8,128)(2,1)S(1)}, bf16[6]{0:T(256)(128)(2,1)S(1)}, bf16[6]{0:T(256)(128)(2,1)S(1)}, bf1...) all-reduce(bf16[1024]{0:T(1024)(128)(2,1)S(1)} %dynamic-slice_reduc, ...), channel_id=1, replica_groups=mesh['seq'=8,'head'=4] {'seq'}, use_global_device_ids=true, to_apply=%region_29.30 | all-reduce | flops 10770 | bytes 43080 | tf_op jit(solution)/shard_map/psum | solution.py:619
  (526 shorter events, 157.0 us)
Async XLA Ops:
  7.2 210.6 %copy-start = (bf16[512,1024]{1,0:T(8,128)(2,1)S(1)}, bf16[512,1024]{1,0:T(8,128)(2,1)}, u32[]{:S(2)}) copy-start(bf16[512,1024]{1,0:T(8,128)(2,1)} %param.37) | copy-start | bytes 3145732
  7.2 59.6 %all-gather.17.cloned.1.call-start = ((), (), s32[]{:S(2)}) async-start(), calls=%async_computation.13 | async-start | bytes 1769472 | tf_op jit(solution)/shard_map/all_gather | solution.py:355
  21.5 6.2 collective-permute-start
  25.2 323.0 %copy-start.83 = (f32[2,512,6]{1,2,0:T(8,128)}, f32[2,512,6]{1,2,0:T(8,128)S(1)}, u32[]{:S(2)}) copy-start(f32[2,512,6]{1,2,0:T(8,128)S(1)} %add_select_fusion) | copy-start | bytes 73732
  35.9 61.6 %all-gather.9.cloned.1.call-start = ((), (), s32[]{:S(2)}) async-start(), calls=%async_computation.4 | async-start | bytes 2359296 | tf_op jit(solution)/shard_map/all_gather | solution.py:380
  42.1 167.3 %all-reduce.17.cloned.1.call-start = ((), (), s32[]{:S(2)}) async-start(), calls=%async_computation.5 | async-start | bytes 4194304 | tf_op jit(solution)/shard_map/psum | solution.py:402
  48.1 16.4 %copy-start.31 = (bf16[2,512,640]{1,2,0:T(8,128)(2,1)S(1)}, bf16[2,512,640]{1,2,0:T(8,128)(2,1)}, u32[]{:S(2)}) copy-start(bf16[2,512,640]{1,2,0:T(8,128)(2,1)} %copy-done.30) | copy-start | bytes 3932164
  111.7 97.7 %copy-start.15 = (bf16[2,512,1024]{2,1,0:T(8,128)(2,1)S(1)}, bf16[2,512,1024]{2,1,0:T(8,128)(2,1)}, u32[]{:S(2)}) copy-start(bf16[2,512,1024]{2,1,0:T(8,128)(2,1)} %param.19) | copy-start | bytes 6291460
  111.7 156.5 %reduce-scatter.9.cloned.1.call-start = ((), (), s32[]{:S(2)}) async-start(), calls=%async_computation.8 | async-start | bytes 2621440 | tf_op jit(solution)/shard_map/reduce_scatter | solution.py:431
  225.3 93.3 %all-gather.13.cloned.1.call-start = ((), (), s32[]{:S(2)}) async-start(), calls=%async_computation.9 | async-start | bytes 2621440 | tf_op jit(solution)/shard_map/all_gather | solution.py:438
  225.4 47.8 %copy-start.135 = (f32[2,128]{1,0:T(2,128)}, f32[2,128]{1,0:T(2,128)S(1)}, u32[]{:S(2)}) copy-start(f32[2,128]{1,0:T(2,128)S(1)} %constant_dynamic-slice_fusion.1) | copy-start | bytes 3076
  225.4 93.2 %copy-start.32 = (bf16[2,512,640]{1,2,0:T(8,128)(2,1)S(1)}, bf16[2,512,640]{1,2,0:T(8,128)(2,1)}, u32[]{:S(2)}) copy-start(bf16[2,512,640]{1,2,0:T(8,128)(2,1)} %copy-done.30) | copy-start | bytes 3932164
  225.4 93.2 %copy-start.78 = (bf16[384,1024]{1,0:T(8,128)(2,1)S(1)}, bf16[384,1024]{1,0:T(8,128)(2,1)}, u32[]{:S(2)}) copy-start(bf16[384,1024]{1,0:T(8,128)(2,1)} %param.31) | copy-start | bytes 2359300
  270.5 52.2 %copy-start.137 = (f32[2,128]{1,0:T(2,128)}, f32[2,128]{1,0:T(2,128)S(1)}, u32[]{:S(2)}) copy-start(f32[2,128]{1,0:T(2,128)S(1)} %broadcast_multiply_fusion.4) | copy-start | bytes 3076
  273.2 94.5 %all-gather.19.cloned.1.call-start = ((), (), s32[]{:S(2)}) async-start(), calls=%async_computation.14 | async-start | bytes 1769472 | tf_op jit(solution)/shard_map/all_gather | solution.py:497
  327.5 75.9 %reduce-scatter.13.cloned.1.call-start = ((), (), s32[]{:S(2)}) async-start(), calls=%async_computation.11 | async-start | bytes 2359296 | tf_op jit(solution)/shard_map/reduce_scatter | solution.py:471
  347.8 111.5 %all-reduce.21.cloned.1.call-start = ((), (), s32[]{:S(2)}) async-start(), calls=%async_computation.16 | async-start | bytes 2097152 | tf_op jit(solution)/shard_map/psum | solution.py:517
  377.5 27.0 %copy-start.146 = (f32[32]{0:T(128)S(1)}, f32[32]{0:T(128)}, u32[]{:S(2)}) copy-start(f32[32]{0:T(128)} %copy-done.145) | copy-start | bytes 388
  406.1 99.2 %reduce-scatter.7.cloned.1.call-start = ((), (), s32[]{:S(2)}) async-start(), calls=%async_computation.6 | async-start | bytes 2621440 | tf_op jit(solution)/shard_map/reduce_scatter | solution.py:411
  408.8 142.7 %reduce-scatter.11.cloned.1.call-start = ((), (), s32[]{:S(2)}) async-start(), calls=%async_computation.10 | async-start | bytes 2621440 | tf_op jit(solution)/shard_map/reduce_scatter | solution.py:571
  415.1 45.3 %copy-start.104 = (f32[640]{0:T(1024)S(1)}, f32[640]{0:T(1024)}, u32[]{:S(2)}) copy-start(f32[640]{0:T(1024)} %copy-done.103) | copy-start | bytes 7684
  415.1 45.3 %copy-start.106 = (f32[640]{0:T(1024)S(1)}, f32[640]{0:T(1024)}, u32[]{:S(2)}) copy-start(f32[640]{0:T(1024)} %copy-done.105) | copy-start | bytes 7684
  415.1 45.3 %copy-start.120 = (pred[2,512]{1,0:T(4,128)(4,1)S(1)}, pred[2,512]{1,0:T(4,128)(4,1)}, u32[]{:S(2)}) copy-start(pred[2,512]{1,0:T(4,128)(4,1)} %copy-done.119) | copy-start | bytes 3076
  415.1 45.3 %copy-start.122 = (pred[2,512]{1,0:T(4,128)(4,1)S(1)}, pred[2,512]{1,0:T(4,128)(4,1)}, u32[]{:S(2)}) copy-start(pred[2,512]{1,0:T(4,128)(4,1)} %copy-done.121) | copy-start | bytes 3076
  468.5 9.6 %collective-permute-start.1 = (f32[2,3,640]{2,0,1:T(2,128)S(1)}, f32[2,3,640]{2,0,1:T(2,128)S(1)}, u32[]{:S(2)}, u32[]{:S(2)}) collective-permute-start(f32[2,3,640]{2,0,1:T(2,128)S(1)} %copy.390), channel_id=1, source_target_pairs={{4,0},{8,4},{12,8},{16,12},{20,16},{24,20},{28,24},{5,1},{9,5},{13... | collective-permute-start | bytes 46088 | tf_op jit(solution)/shard_map/ppermute | solution.py:26
  490.3 108.6 %all-gather.11.cloned.1.call-start = ((), (), s32[]{:S(2)}) async-start(), calls=%async_computation.7 | async-start | bytes 2621440 | tf_op jit(solution)/shard_map/all_gather | solution.py:598
  507.7 209.9 %all-reduce.19.cloned.1.call-start = ((), (), s32[]{:S(2)}) async-start(), calls=%async_computation.15 | async-start | bytes 14155776 | tf_op jit(solution)/shard_map/psum | solution.py:620
  529.7 21.7 %slice-start = ((bf16[2,512,640]{1,2,0:T(8,128)(2,1)}), bf16[2,512,256]{1,2,0:T(8,128)(2,1)S(1)}, s32[]{:S(2)}) async-start(bf16[2,512,640]{1,2,0:T(8,128)(2,1)} %copy-done.50), calls=%async_computation.17 | async-start | bytes 1048576 | tf_op jit(solution)/shard_map/slice | solution.py:539
  529.7 252.6 %all-gather.15.cloned.1.call-start = ((), (), s32[]{:S(2)}) async-start(), calls=%async_computation.12 | async-start | bytes 2621440 | tf_op jit(solution)/shard_map/all_gather | solution.py:599
  599.6 122.8 %copy-start.134 = (bf16[4,640]{1,0:T(4,128)(2,1)}, bf16[4,640]{1,0:T(4,128)(2,1)S(1)}, u32[]{:S(2)}) copy-start(bf16[4,640]{1,0:T(4,128)(2,1)S(1)} %maximum_convert_fusion) | copy-start | bytes 15364
  732.2 22.4 %slice-start.1 = ((bf16[4,640]{1,0:T(4,128)(2,1)}), bf16[4,384]{1,0:T(4,128)(2,1)S(1)}, s32[]{:S(2)}) async-start(bf16[4,640]{1,0:T(4,128)(2,1)} %copy-done.134), calls=%async_computation.18 | async-start | bytes 6144 | tf_op jit(solution)/shard_map/slice | solution.py:626
  732.2 50.2 %copy-start.63 = (bf16[2,512,1024]{2,1,0:T(8,128)(2,1)S(1)}, bf16[2,512,1024]{2,1,0:T(8,128)(2,1)}, u32[]{:S(2)}) copy-start(bf16[2,512,1024]{2,1,0:T(8,128)(2,1)} %all-gather.11.cloned.1.call-done) | copy-start | bytes 6291460
  (150 other events, 454.6 us)
Sparse Core Ops, SparseCore 0:
  36.0 30.7 all-gather.16
  69.3 28.1 all-gather.8
  111.9 97.4 all-reduce.16
  225.4 42.7 reduce-scatter.8
  273.3 45.2 all-gather.12
  327.6 24.4 all-gather.18
  355.9 47.3 reduce-scatter.12
  407.1 52.1 all-reduce.20
  462.1 43.1 reduce-scatter.6
  508.2 43.2 reduce-scatter.10
  553.6 45.2 all-gather.10
  604.6 112.9 all-reduce.18
  719.8 46.5 all-gather.14

commit v2 on v1

--- a/solution.py
+++ b/solution.py
@@ -261,6 +261,176 @@
         ],
         compiler_params=pltpu.CompilerParams(vmem_limit_bytes=48 * 1024 * 1024),
     )(low, high, query, grad, place, begin, stat, dots, keyval, keyval_t)
+
+
+def head_kernel(ways, scatter, gather, part_ref, out_ref, landed, sends, arrivals):
+    me = lax.axis_index("head")
+    rows = part_ref.shape[0]
+    share = part_ref.shape[1] // ways if scatter else part_ref.shape[1]
+    barrier = pltpu.get_barrier_semaphore()
+    for hop in range(1, ways):
+        pl.semaphore_signal(
+            barrier,
+            inc=1,
+            device_id={"head": lax.rem(me + hop, ways)},
+            device_id_type=pl.DeviceIdType.MESH,
+        )
+    pl.semaphore_wait(barrier, ways - 1)
+    mine = pl.ds(pl.multiple_of(me * share, 16), share)
+    order = (2, 1, 3) if ways == 4 else tuple(range(1, ways))
+    if scatter:
+        copies = []
+        for hop in order:
+            peer = lax.rem(me + hop, ways)
+            copy = pltpu.make_async_remote_copy(
+                src_ref=part_ref.at[:, pl.ds(pl.multiple_of(peer * share, 16), share), :],
+                dst_ref=landed.at[hop - 1],
+                send_sem=sends.at[hop - 1],
+                recv_sem=arrivals.at[hop - 1],
+                device_id={"head": peer},
+                device_id_type=pl.DeviceIdType.MESH,
+            )
+            copy.start()
+            copies.append(copy)
+        for copy in copies:
+            copy.wait()
+        place = mine if gather else pl.ds(0, share)
+        for row in range(rows):
+            total = part_ref[row, mine, :].astype(jnp.float32)
+            for hop in range(1, ways):
+                total = total + landed[hop - 1, row].astype(jnp.float32)
+            out_ref[row, place, :] = total.astype(out_ref.dtype)
+    else:
+        for row in range(rows):
+            out_ref[row, mine, :] = part_ref[row]
+    if gather:
+        copies = []
+        for hop in order:
+            copy = pltpu.make_async_remote_copy(
+                src_ref=out_ref.at[:, mine, :],
+                dst_ref=out_ref.at[:, mine, :],
+                send_sem=sends.at[ways + hop - 1],
+                recv_sem=arrivals.at[ways + hop - 1],
+                device_id={"head": lax.rem(me + hop, ways)},
+                device_id_type=pl.DeviceIdType.MESH,
+            )
+            copy.start()
+            copies.append(copy)
+        for copy in copies:
+            copy.wait()
+
+
+def head_exchange(part, number, scatter, gather):
+    ways = lax.axis_size("head")
+    rows, length, width = part.shape
+    share = length // ways if scatter else length
+    landed = (ways - 1, rows, share, width) if scatter else (1, 1, 16, 128)
+    return pl.pallas_call(
+        partial(head_kernel, ways, scatter, gather),
+        out_shape=jax.ShapeDtypeStruct((rows, share * ways if gather else share, width), part.dtype),
+        in_specs=[pl.BlockSpec(memory_space=pltpu.VMEM)],
+        out_specs=pl.BlockSpec(memory_space=pltpu.VMEM),
+        scratch_shapes=[
+            pltpu.VMEM(landed, part.dtype),
+            pltpu.SemaphoreType.DMA((2 * ways,)),
+            pltpu.SemaphoreType.DMA((2 * ways,)),
+        ],
+        compiler_params=pltpu.CompilerParams(
+            collective_id=number, has_side_effects=True, vmem_limit_bytes=32 * 1024 * 1024
+        ),
+    )(part)
+
+
+def grads_kernel(ways, part_ref, out_ref, paired, landed, spread, sends, arrivals):
+    me = lax.axis_index("seq")
+    core = lax.rem(me, 2)
+    chips = ways // 2
+    chip = me // 2
+    sibling = me + 1 - 2 * core
+    half = part_ref.shape[0] // 2
+    share = half // chips
+    barrier = pltpu.get_barrier_semaphore()
+    peers = [lax.rem(chip + hop, chips) * 2 + core for hop in range(1, chips)]
+    for peer in peers + [sibling]:
+        pl.semaphore_signal(
+            barrier, inc=1, device_id={"seq": peer}, device_id_type=pl.DeviceIdType.MESH
+        )
+    pl.semaphore_wait(barrier, chips)
+
+    def send(source, target, number, peer):
+        copy = pltpu.make_async_remote_copy(
+            src_ref=source,
+            dst_ref=target,
+            send_sem=sends.at[number],
+            recv_sem=arrivals.at[number],
+            device_id={"seq": peer},
+            device_id_type=pl.DeviceIdType.MESH,
+        )
+        copy.start()
+        return copy
+
+    def span(start, size):
+        return pl.ds(pl.multiple_of(start, 16), size)
+
+    own = core * half
+    send(part_ref.at[span((1 - core) * half, half), :], landed, 0, sibling).wait()
+
+    @pl.loop(0, half // 16)
+    def _(tile):
+        here = span(tile * 16, 16)
+        paired[here, :] = (
+            part_ref[span(own + tile * 16, 16), :].astype(jnp.float32)
+            + landed[here, :].astype(jnp.float32)
+        ).astype(paired.dtype)
+
+    copies = []
+    for hop in range(1, chips):
+        to = lax.rem(chip + hop, chips)
+        copies.append(
+            send(paired.at[span(to * share, share), :], spread.at[hop - 1], hop, peers[hop - 1])
+        )
+    for copy in copies:
+        copy.wait()
+    mine = own + chip * share
+
+    @pl.loop(0, share // 16)
+    def _(tile):
+        here = span(tile * 16, 16)
+        total = paired[span(chip * share + tile * 16, 16), :].astype(jnp.float32)
+        for hop in range(1, chips):
+            total = total + spread[hop - 1, here, :].astype(jnp.float32)
+        out_ref[span(mine + tile * 16, 16), :] = total.astype(out_ref.dtype)
+
+    place = out_ref.at[span(mine, share), :]
+    copies = [
+        send(place, place, chips + hop, peers[hop - 1]) for hop in range(1, chips)
+    ]
+    for copy in copies:
+        copy.wait()
+    place = out_ref.at[span(own, half), :]
+    send(place, place, chips, sibling).wait()
+
+
+def grads_sum(part, number):
+    ways = lax.axis_size("seq")
+    rows, width = part.shape
+    chips = ways // 2
+    return pl.pallas_call(
+        partial(grads_kernel, ways),
+        out_shape=jax.ShapeDtypeStruct(part.shape, part.dtype),
+        in_specs=[pl.BlockSpec(memory_space=pltpu.VMEM)],
+        out_specs=pl.BlockSpec(memory_space=pltpu.VMEM),
+        scratch_shapes=[
+            pltpu.VMEM((rows // 2, width), part.dtype),
+            pltpu.VMEM((rows // 2, width), part.dtype),
+            pltpu.VMEM((chips - 1, rows // ways, width), part.dtype),
+            pltpu.SemaphoreType.DMA((2 * chips,)),
+            pltpu.SemaphoreType.DMA((2 * chips,)),
+        ],
+        compiler_params=pltpu.CompilerParams(
+            collective_id=number, has_side_effects=True, vmem_limit_bytes=48 * 1024 * 1024
+        ),
+    )(part)
 
 
 def local(
@@ -399,9 +569,9 @@
     attend_part = jnp.einsum(
         "rtc,cd->rtd", attended_low, attend_down, preferred_element_type=jnp.float32
     )
-    mixed_sum = lax.psum((mixer_part + attend_part).astype(jnp.bfloat16), "head").astype(
-        jnp.float32
-    )
+    mixed_sum = head_exchange(
+        (mixer_part + attend_part).astype(jnp.bfloat16), 1, True, True
+    ).astype(jnp.float32)
     middle = inputs + mixed_sum
     normed_two, scaled_two, gained_two = norm_forward(middle, ffn_gain)
     middle_low = gained_two.astype(jnp.bfloat16)
@@ -428,14 +598,14 @@
     middle_low_part = jnp.einsum(
         "rtkf,dkf->rtd", ffn_pre_grad, ffn_in, preferred_element_type=jnp.float32
     )
-    low_grad_share = lax.psum_scatter(
-        middle_low_part.astype(jnp.bfloat16), "head", scatter_dimension=1, tiled=True
+    low_grad_share = head_exchange(
+        middle_low_part.astype(jnp.bfloat16), 2, True, False
     ).astype(jnp.float32)
     norm_back_share, ffn_gain_part = norm_backward(
         low_grad_share, share_of(normed_two), share_of(scaled_two), ffn_gain
     )
     middle_grad_share = share_of(cotangent).astype(jnp.float32) + norm_back_share
-    mixed_low = lax.all_gather(middle_grad_share.astype(jnp.bfloat16), "head", axis=1, tiled=True)
+    mixed_low = head_exchange(middle_grad_share.astype(jnp.bfloat16), 3, False, True)
     gated_grad = jnp.einsum(
         "rtd,cd->rtc", mixed_low, mixer_down, preferred_element_type=jnp.float32
     ).reshape(row_count, length, head_count, head_dim)
@@ -513,10 +683,20 @@
         axis=2,
     )
     pre_grad = act_grad * silu_slope(conv_pre)
-    state_total, keyval_total = (
-        lax.psum(pre_grad[:, :, inner_width:].astype(jnp.bfloat16), "head").astype(jnp.float32),
-        lax.psum(keyval_part.astype(jnp.bfloat16), "head").astype(jnp.float32),
-    )
+    state_width = pre_grad.shape[2] - inner_width
+    shared_total = head_exchange(
+        jnp.concatenate(
+            [
+                pre_grad[:, :, inner_width:].astype(jnp.bfloat16),
+                keyval_part.reshape(row_count, length, 2 * kv_total * ATT_DIM).astype(jnp.bfloat16),
+            ],
+            axis=2,
+        ),
+        4,
+        True,
+        True,
+    ).astype(jnp.float32)
+    state_total, keyval_total = shared_total[..., :state_width], shared_total[..., state_width:]
     pre_grad = jnp.concatenate([pre_grad[:, :, :inner_width], state_total], axis=2)
     padded_grad = jnp.zeros((row_count, length + tap_count - 1, pre_grad.shape[2]), jnp.float32)
     conv_grads = []
@@ -567,72 +747,70 @@
     norm_rider = jnp.sum(head_part * normed_one, axis=(0, 1)) + jnp.sum(
         common_share * normed_share, axis=(0, 1)
     )
-    head_share, ffn_gain_total, norm_gain_total = (
-        lax.psum_scatter(
-            head_part.astype(jnp.bfloat16), "head", scatter_dimension=1, tiled=True
-        ).astype(jnp.float32),
-        lax.psum_scatter(
-            jnp.broadcast_to(ffn_gain_part[None, None, :], (1, head_ways, model_width)).astype(
-                jnp.bfloat16
-            ),
-            "head",
-            scatter_dimension=1,
-            tiled=True,
-        ).astype(jnp.float32),
-        lax.psum_scatter(
-            jnp.broadcast_to(norm_rider[None, None, :], (1, head_ways, model_width)).astype(
-                jnp.bfloat16
-            ),
-            "head",
-            scatter_dimension=1,
-            tiled=True,
-        ).astype(jnp.float32),
-    )
-    ffn_gain_grad = ffn_gain_total.reshape(model_width)
-    norm_gain_grad = norm_gain_total.reshape(model_width)
+    head_share = head_exchange(head_part.astype(jnp.bfloat16), 5, True, False).astype(jnp.float32)
+    gains = jnp.pad(
+        jnp.stack([ffn_gain_part, norm_rider]).astype(jnp.bfloat16)[None], ((0, 0), (0, 14), (0, 0))
+    )
+    gains = jnp.sum(
+        head_exchange(gains, 6, False, True)
+        .astype(jnp.float32)
+        .reshape(head_ways, 16, model_width)[:, :2],
+        axis=0,
+    )
     norm_back_share_one, unused_gain = norm_backward(
         head_share + common_share, normed_share, share_of(scaled_one), norm_gain
     )
     token_share = (middle_grad_share + norm_back_share_one).astype(jnp.bfloat16)
     output, token_grad = (
         lax.all_gather(output_share, "head", axis=1, tiled=True),
-        lax.all_gather(token_share, "head", axis=1, tiled=True),
-    )
-    (
-        norm_gain_sum,
-        mixer_proj_sum,
-        state_proj_sum,
-        step_proj_sum,
-        step_bias_sum,
-        decay_log_sum,
-        skip_gain_sum,
-        conv_mixer_sum,
-        conv_state_sum,
-        mixer_down_sum,
-        query_proj_sum,
-        keyval_proj_sum,
-        attend_down_sum,
-        ffn_gain_sum,
-        ffn_in_sum,
-        ffn_down_sum,
-    ) = (
-        lax.psum(norm_gain_grad.astype(jnp.bfloat16), "seq").astype(jnp.float32),
-        lax.psum(mixer_proj_grad.astype(jnp.bfloat16), "seq").astype(jnp.float32),
-        lax.psum(state_proj_grad.astype(jnp.bfloat16), "seq").astype(jnp.float32),
-        lax.psum(step_proj_grad.astype(jnp.bfloat16), "seq").astype(jnp.float32),
-        lax.psum(step_bias_grad.astype(jnp.bfloat16), "seq").astype(jnp.float32),
-        lax.psum(decay_log_grad.astype(jnp.bfloat16), "seq").astype(jnp.float32),
-        lax.psum(skip_gain_grad.astype(jnp.bfloat16), "seq").astype(jnp.float32),
-        lax.psum(conv_weight_grad[:, :inner_width].astype(jnp.bfloat16), "seq").astype(jnp.float32),
-        lax.psum(conv_weight_grad[:, inner_width:].astype(jnp.bfloat16), "seq").astype(jnp.float32),
-        lax.psum(mixer_down_grad.astype(jnp.bfloat16), "seq").astype(jnp.float32),
-        lax.psum(query_proj_grad.astype(jnp.bfloat16), "seq").astype(jnp.float32),
-        lax.psum(keyval_proj_grad.astype(jnp.bfloat16), "seq").astype(jnp.float32),
-        lax.psum(attend_down_grad.astype(jnp.bfloat16), "seq").astype(jnp.float32),
-        lax.psum(ffn_gain_grad.astype(jnp.bfloat16), "seq").astype(jnp.float32),
-        lax.psum(ffn_in_grad.astype(jnp.bfloat16), "seq").astype(jnp.float32),
-        lax.psum(ffn_down_grad.astype(jnp.bfloat16), "seq").astype(jnp.float32),
-    )
+        head_exchange(token_share, 7, False, True),
+    )
+    def tall(values):
+        return jnp.pad(values, ((0, model_width - values.shape[0]), (0, 0)))
+
+    small = [
+        step_proj_grad,
+        gains.T,
+        tall(conv_weight_grad[:, :inner_width].T),
+        tall(conv_weight_grad[:, inner_width:].T),
+        tall(jnp.stack([step_bias_grad, decay_log_grad, skip_gain_grad], axis=1)),
+    ]
+    small = jnp.concatenate(small, axis=1)
+    small = jnp.pad(small, ((0, 0), (0, 128 - small.shape[1])))
+    down_grads = [ffn_down_grad, mixer_down_grad, attend_down_grad]
+    pieces = [
+        mixer_proj_grad.reshape(model_width, -1),
+        ffn_in_grad.reshape(model_width, -1),
+        query_proj_grad,
+        state_proj_grad,
+        keyval_proj_grad.reshape(model_width, -1),
+        tall(jnp.concatenate([grad.astype(jnp.bfloat16) for grad in down_grads], axis=0)),
+        small,
+    ]
+    summed = grads_sum(jnp.concatenate([piece.astype(jnp.bfloat16) for piece in pieces], axis=1), 8)
+    parts = []
+    begin = 0
+    for piece in pieces:
+        parts.append(summed[:, begin : begin + piece.shape[1]].astype(jnp.float32))
+        begin += piece.shape[1]
+    mixer_proj_sum = parts[0].reshape(mixer_proj_grad.shape)
+    ffn_in_sum = parts[1].reshape(ffn_in_grad.shape)
+    query_proj_sum, state_proj_sum = parts[2], parts[3]
+    keyval_proj_sum = parts[4].reshape(keyval_proj_grad.shape)
+    down_at = (ffn_down_grad.shape[0], ffn_down_grad.shape[0] + mixer_down_grad.shape[0])
+    ffn_down_sum, mixer_down_sum, attend_down_sum = jnp.split(
+        parts[5][: down_at[1] + attend_down_grad.shape[0]], down_at, axis=0
+    )
+    small_sum = parts[6]
+    at = head_count
+    step_proj_sum = small_sum[:, :at]
+    ffn_gain_sum, norm_gain_sum = small_sum[:, at], small_sum[:, at + 1]
+    at += 2
+    conv_mixer_sum = small_sum[:inner_width, at : at + tap_count].T
+    at += tap_count
+    conv_state_sum = small_sum[: 2 * states, at : at + tap_count].T
+    at += tap_count
+    step_bias_sum, decay_log_sum, skip_gain_sum = (small_sum[:head_count, at + i] for i in range(3))
     return (
         output,
         token_grad,

time: 802 us -> 846 us (1.055)
  Pallas kernels: 8.74 us -> 476 us
  waiting for transfers between devices: 465 us -> 30.6 us
  blocking collectives: 56.3 us -> 10.1 us
  local copies, waits for them, and re-layouts: 70.2 us -> 107 us
    pallas_call x0 -> x8, Pallas kernels: none -> 466 us  [the longest x7 361 us: head_exchange(): pl.pallas_call(partial(head_kernel, ways, scatter, gather), out_shape=jax...]
    psum x3 -> x0, waiting for transfers between devices: 257 us -> none  [the longest x1 118 us: local(): lax.psum(mixer_proj_grad.astype(jnp.bfloat16), 'seq').astype(jnp.float32)]
    reduce_scatter x2 -> x0, waiting for transfers between devices: 61.4 us -> none  [the longest x1 42.9 us: local(): lax.psum_scatter(middle_low_part.astype(jnp.bfloat16), 'head', scatter_di...]
    all_gather x2 -> x0, waiting for transfers between devices: 45.4 us -> none  [the longest x1 45.4 us: local(): lax.all_gather(middle_grad_share.astype(jnp.bfloat16), 'head', axis=1, ti...]
    all_gather x1, waiting for transfers between devices: 40.9 us -> 0.01 us  [local(): lax.all_gather(output_share, 'head', axis=1, tiled=True)]
    psum x1 -> x0, blocking collectives: 23.2 us -> none  [local(): lax.psum(norm_gain_grad.astype(jnp.bfloat16), 'seq').astype(jnp.float32)]
    unnamed x1 -> x0, blocking collectives: 19.5 us -> none
    reshape x0 -> x4, local copies, waits for them, and re-layouts: none -> 16.3 us  [the longest x1 6.57 us: local(): ffn_in_sum = parts[1].reshape(ffn_in_grad.shape)]
  transfers between devices with their start and end apart: 15 -> 8, of which waited for: 11 -> 2; matrix products, arithmetic and copies ran while one was open for 20% -> 26% of each run, Pallas kernels for 1% -> 35%
where the time goes in v2:
time: 846 us; the launch traced here: 831 us
  Pallas kernels  476 us (56%)
  matrix products  114 us (13%)
  local copies, waits for them, and re-layouts  107 us (13%)
  other arithmetic  73.2 us (9%)
  waiting for transfers between devices  30.6 us (4%)
  between operations  16.2 us (2%)
  blocking collectives  10.1 us (1%)
    pallas_call x7, Pallas kernels, head_exchange(): pl.pallas_call(partial(head_kernel, ways, scatter, gather), out_shape=jax...  361 us
    pallas_call x1, Pallas kernels, grads_sum(): pl.pallas_call(partial(grads_kernel, ways), out_shape=jax.ShapeDtypeStruc...  105 us
    unnamed x305, local copies, waits for them, and re-layouts  40.2 us
    dot_general x3, matrix products, state_output(): jnp.einsum('rtsh,rshp->rthp', gram_mat[..., None] * decay_mat, drive_in,...  22.2 us
    reduce_scatter x1, waiting for transfers between devices, local(): lax.psum_scatter(keyval_grads, 'seq', scatter_dimension=1, tiled=True)  18.9 us
  transfers between devices with their start and end apart: 8, of which 2 were waited for; matrix products, arithmetic and copies ran while one was open for 26% of the time, Pallas kernels for 35%

profile of v2, /device:TPU:0, one launch (start us, length us, event | category | flops | bytes accessed | tf_op | source)
XLA Modules:
  0.0 830.8 jit_solution(1342427027237556833)
XLA Ops:
  40.9 10.1 %all_gather.22 = bf16[8,2,6]{2,1,0:T(2,128)(2,1)S(1)} all-gather(bf16[1,2,6]{2,1,0:T(2,128)(2,1)S(1)} %fusion.219), channel_id=1, replica_groups=mesh['seq'=8,'head'=4] {'seq'}, dimensions={0}, use_global_device_ids=true | all-gather | bytes 216 | tf_op jit(solution)/shard_map/all_gather | solution.py:523
  71.7 7.2 multiply_convert_fusion.7
  78.9 11.6 %all-gather.7.cloned.1.call-done = bf16[2,4096,128]{1,2,0:T(8,128)(2,1)} async-done(((bf16[2,512,128]{1,2,0:T(8,128)(2,1)}), bf16[2,4096,128]{1,2,0:T(8,128)(2,1)}) %all-gather.7.cloned.1.call-update) | async-done | bytes 2097168 | tf_op jit(solution)/shard_map/all_gather | solution.py:550
  90.6 4.1 copy.443.kv_ref
  97.8 3.6 shard_map.322
  104.2 96.3 %shard_map.323 = bf16[2,512,1024]{2,1,0:T(8,128)(2,1)S(1)} custom-call(bf16[2,512,1024]{2,1,0:T(8,128)(2,1)S(1)} %add_convert_fusion.part_ref), custom_call_target="tpu_custom_call" | custom-call | tf_op jit(solution)/shard_map/pallas_call | solution.py:328
  213.7 39.6 %shard_map.324 = bf16[2,128,1024]{2,1,0:T(8,128)(2,1)S(1)} custom-call(bf16[2,512,1024]{2,1,0:T(8,128)(2,1)S(1)} %bitcast_convert_fusion.1.part_ref), custom_call_target="tpu_custom_call" | custom-call | tf_op jit(solution)/shard_map/pallas_call | solution.py:328
  254.4 48.6 %shard_map.325 = bf16[2,512,1024]{2,1,0:T(8,128)(2,1)S(1)} custom-call(bf16[2,128,1024]{2,1,0:T(8,128)(2,1)S(1)} %fusion.182.part_ref), custom_call_target="tpu_custom_call" | custom-call | tf_op jit(solution)/shard_map/pallas_call | solution.py:328
  309.7 5.5 multiply_reduce_fusion.3
  318.5 6.5 bitcast_convert_fusion
  325.0 4.0 copy.531
  329.6 3.1 fusion.134
  337.9 5.7 shard_map.326
  345.7 4.1 copy.459
  369.9 5.4 fusion.6
  375.3 9.7 %fusion.11 = (f32[2,512,6]{1,2,0:T(8,128)}, f32[2,512,6]{1,2,0:T(8,128)}, bf16[2,512,512]{2,1,0:T(8,128)(2,1)}) fusion(f32[2,512,6]{1,2,0:T(8,128)S(1)} %bitcast.423, f32[2,512,512]{2,1,0:T(8,128)S(1)} %copy-done.54, pred[2,512,512]{2,1,0:T(8,128)(4,1)S(1)} %copy-done.70, f32[2,512,6,64]{1,3,2,0:T(8,128)S(1)} %bitcast.395, ...), kind=kOutput, calls=%fused_computation.12 | convolution fusion | flops 437112832 | bytes 6914048 | tf_op jit(solution)/shard_map/transpose(jvp(rtsh,rshp->rthp))/dot_general | solution.py:125
  400.6 4.5 maximum_multiply_fusion
  419.9 18.9 %reduce-scatter.5.cloned.1.call-done = bf16[2,512,128]{1,2,0:T(8,128)(2,1)} async-done(((bf16[2,4096,128]{1,2,0:T(8,128)(2,1)}), bf16[2,512,128]{1,2,0:T(8,128)(2,1)}) %reduce-scatter.5.cloned.1.call-update) | async-done | bytes 262160 | tf_op jit(solution)/shard_map/reduce_scatter | solution.py:641
  445.4 79.6 %shard_map.327 = bf16[2,512,512]{2,1,0:T(8,128)(2,1)S(1)} custom-call(bf16[2,512,512]{2,1,0:T(8,128)(2,1)S(1)} %pad_maximum_fusion.6.part_ref), custom_call_target="tpu_custom_call" | custom-call | tf_op jit(solution)/shard_map/pallas_call | solution.py:328
  526.0 3.7 fusion.30
  547.1 3.2 bitcast_convert_fusion.2
  552.9 6.4 multiply_reduce_fusion
  559.3 42.3 %shard_map.328 = bf16[2,128,1024]{2,1,0:T(8,128)(2,1)S(1)} custom-call(bf16[2,512,1024]{2,1,0:T(8,128)(2,1)S(1)} %get-tuple-element.196.part_ref), custom_call_target="tpu_custom_call" | custom-call | tf_op jit(solution)/shard_map/pallas_call | solution.py:328
  603.2 15.7 %shard_map.330 = bf16[1,64,1024]{2,1,0:T(8,128)(2,1)S(1)} custom-call(bf16[1,16,1024]{2,1,0:T(8,128)(2,1)S(1)} %fusion.185.part_ref), custom_call_target="tpu_custom_call" | custom-call | tf_op jit(solution)/shard_map/pallas_call | solution.py:328
  631.6 3.6 fusion.85
  637.6 105.4 %shard_map.331 = bf16[1024,3584]{1,0:T(8,128)(2,1)} custom-call(bf16[1024,3584]{1,0:T(8,128)(2,1)} %pad_dynamic-update-slice_fusion.part_ref), custom_call_target="tpu_custom_call" | custom-call | tf_op jit(solution)/shard_map/pallas_call | solution.py:418
  743.1 5.1 slice_convert_fusion
  754.1 38.7 %shard_map.329 = bf16[2,512,1024]{2,1,0:T(8,128)(2,1)S(1)} custom-call(bf16[2,128,1024]{2,1,0:T(8,128)(2,1)S(1)} %add_convert_fusion.1.part_ref), custom_call_target="tpu_custom_call" | custom-call | tf_op jit(solution)/shard_map/pallas_call | solution.py:328
  802.2 3.3 slice_convert_fusion.3
  805.5 5.2 reshape.603
  810.7 6.6 reshape.607
  819.2 3.2 copy.575
  (492 shorter events, 204.0 us)
Async XLA Ops:
  7.2 59.3 %all-gather.11.cloned.1.call-start = ((), (), s32[]{:S(2)}) async-start(), calls=%async_computation.6 | async-start | bytes 1769472 | tf_op jit(solution)/shard_map/all_gather | solution.py:525
  9.6 8.7 %copy-start.95 = (f32[2,512]{1,0:T(2,128)}, f32[2,512]{1,0:T(2,128)S(1)}, u32[]{:S(2)}) copy-start(f32[2,512]{1,0:T(2,128)S(1)} %add_rsqrt_fusion.1) | copy-start | bytes 12292
  11.4 11.0 %copy-start.34 = (bf16[2,512,256]{2,1,0:T(8,128)(2,1)}, bf16[2,512,256]{2,1,0:T(8,128)(2,1)S(1)}, u32[]{:S(2)}) copy-start(bf16[2,512,256]{2,1,0:T(8,128)(2,1)S(1)} %convolution_convert_fusion.1) | copy-start | bytes 1572868
  15.1 7.0 collective-permute-start
  17.9 13.5 %copy-start.100 = (s32[2,512]{1,0:T(2,128)}, s32[2,512]{1,0:T(2,128)S(1)}, u32[]{:S(2)}) copy-start(s32[2,512]{1,0:T(2,128)S(1)} %get-tuple-element.186) | copy-start | bytes 12292
  21.2 49.4 %copy-start.76 = (f32[2,6,512]{2,1,0:T(8,128)}, f32[2,6,512]{2,1,0:T(8,128)S(1)}, u32[]{:S(2)}) copy-start(f32[2,6,512]{2,1,0:T(8,128)S(1)} %fusion.117) | copy-start | bytes 73732
  31.4 59.2 %all-gather.7.cloned.1.call-start = ((), (), s32[]{:S(2)}) async-start(), calls=%async_computation.2 | async-start | bytes 2359296 | tf_op jit(solution)/shard_map/all_gather | solution.py:550
  35.2 16.3 %copy-start.105 = (s32[512]{0:T(512)S(1)}, s32[512]{0:T(512)}, u32[]{:S(2)}) copy-start(s32[512]{0:T(512)} %copy-done.104) | copy-start | bytes 6148
  38.4 15.8 %copy-start.102 = (s32[2,512]{1,0:T(2,128)S(1)}, s32[2,512]{1,0:T(2,128)}, u32[]{:S(2)}) copy-start(s32[2,512]{1,0:T(2,128)} %copy-done.101) | copy-start | bytes 12292
  38.4 16.6 %copy-start.130 = (f32[32]{0:T(128)S(1)}, f32[32]{0:T(128)}, u32[]{:S(2)}) copy-start(f32[32]{0:T(128)} %copy-done.129) | copy-start | bytes 388
  39.2 17.1 %copy-start.74 = (bf16[1024,128]{1,0:T(8,128)(2,1)S(1)}, bf16[1024,128]{1,0:T(8,128)(2,1)}, u32[]{:S(2)}) copy-start(bf16[1024,128]{1,0:T(8,128)(2,1)} %param.32) | copy-start | bytes 786436
  39.2 17.1 %copy-start.119 = (f32[1024]{0:T(1024)S(1)}, f32[1024]{0:T(1024)}, u32[]{:S(2)}) copy-start(f32[1024]{0:T(1024)} %param.22) | copy-start | bytes 12292
  39.2 350.3 %all-gather.13.cloned.1.call-start = ((), (), s32[]{:S(2)}) async-start(), calls=%async_computation.7 | async-start | bytes 1769472 | tf_op jit(solution)/shard_map/all_gather | solution.py:667
  104.2 96.3 %copy-start.14 = (bf16[2,512,1024]{2,1,0:T(8,128)(2,1)S(1)}, bf16[2,512,1024]{2,1,0:T(8,128)(2,1)}, u32[]{:S(2)}) copy-start(bf16[2,512,1024]{2,1,0:T(8,128)(2,1)} %param.19) | copy-start | bytes 6291460
  203.3 50.9 %copy-start.121 = (f32[2,128]{1,0:T(2,128)}, f32[2,128]{1,0:T(2,128)S(1)}, u32[]{:S(2)}) copy-start(f32[2,128]{1,0:T(2,128)S(1)} %constant_dynamic-slice_fusion.2) | copy-start | bytes 3076
  204.9 49.2 %copy-start.36 = (f32[2,512,1024]{2,1,0:T(8,128)}, f32[2,512,1024]{2,1,0:T(8,128)S(1)}, u32[]{:S(2)}) copy-start(f32[2,512,1024]{2,1,0:T(8,128)S(1)} %broadcast_multiply_fusion) | copy-start | bytes 12582916
  254.1 48.9 %copy-start.123 = (f32[2,128]{1,0:T(2,128)}, f32[2,128]{1,0:T(2,128)S(1)}, u32[]{:S(2)}) copy-start(f32[2,128]{1,0:T(2,128)S(1)} %broadcast_multiply_fusion.4) | copy-start | bytes 3076
  318.4 120.3 %reduce-scatter.5.cloned.1.call-start = ((), (), s32[]{:S(2)}) async-start(), calls=%async_computation.5 | async-start | bytes 2359296 | tf_op jit(solution)/shard_map/reduce_scatter | solution.py:641
  363.1 266.1 %reduce-scatter.3.cloned.1.call-start = ((), (), s32[]{:S(2)}) async-start(), calls=%async_computation.3 | async-start | bytes 2621440 | tf_op jit(solution)/shard_map/reduce_scatter | solution.py:581
  385.0 434.3 %all-gather.9.cloned.1.call-start = ((), (), s32[]{:S(2)}) async-start(), calls=%async_computation.4 | async-start | bytes 2621440 | tf_op jit(solution)/shard_map/all_gather | solution.py:765
  417.1 22.7 %copy-start.131 = (f32[32]{0:T(128)S(1)}, f32[32]{0:T(128)}, u32[]{:S(2)}) copy-start(f32[32]{0:T(128)} %copy-done.129) | copy-start | bytes 388
  445.3 80.6 %copy-start.18 = (bf16[2,512,384]{2,1,0:T(8,128)(2,1)S(1)}, bf16[2,512,384]{2,1,0:T(8,128)(2,1)}, u32[]{:S(2)}) copy-start(bf16[2,512,384]{2,1,0:T(8,128)(2,1)} %copy-done.17) | copy-start | bytes 2359300
  445.3 80.6 %copy-start.33 = (f32[2,512,384]{2,1,0:T(8,128)S(1)}, f32[2,512,384]{2,1,0:T(8,128)}, u32[]{:S(2)}) copy-start(f32[2,512,384]{2,1,0:T(8,128)} %slice.281) | copy-start | bytes 4718596
  445.3 80.6 %copy-start.35 = (bf16[2,512,256]{2,1,0:T(8,128)(2,1)S(1)}, bf16[2,512,256]{2,1,0:T(8,128)(2,1)}, u32[]{:S(2)}) copy-start(bf16[2,512,256]{2,1,0:T(8,128)(2,1)} %copy-done.34) | copy-start | bytes 1572868
  445.3 80.6 %copy-start.91 = (pred[2,512]{1,0:T(4,128)(4,1)S(1)}, pred[2,512]{1,0:T(4,128)(4,1)}, u32[]{:S(2)}) copy-start(pred[2,512]{1,0:T(4,128)(4,1)} %copy-done.89) | copy-start | bytes 3076
  445.3 80.6 %copy-start.94 = (pred[2,512]{1,0:T(4,128)(4,1)S(1)}, pred[2,512]{1,0:T(4,128)(4,1)}, u32[]{:S(2)}) copy-start(pred[2,512]{1,0:T(4,128)(4,1)} %copy-done.92) | copy-start | bytes 3076
  445.3 80.6 %copy-start.108 = (pred[2,512]{1,0:T(4,128)(4,1)S(1)}, pred[2,512]{1,0:T(4,128)(4,1)}, u32[]{:S(2)}) copy-start(pred[2,512]{1,0:T(4,128)(4,1)} %copy-done.106) | copy-start | bytes 3076
  445.4 80.6 %copy-start.111 = (pred[2,512]{1,0:T(4,128)(4,1)S(1)}, pred[2,512]{1,0:T(4,128)(4,1)}, u32[]{:S(2)}) copy-start(pred[2,512]{1,0:T(4,128)(4,1)} %copy-done.109) | copy-start | bytes 3076
  536.0 6.9 collective-permute-start.1
  559.3 43.9 %copy-start.37 = (f32[2,512,1024]{2,1,0:T(8,128)}, f32[2,512,1024]{2,1,0:T(8,128)S(1)}, u32[]{:S(2)}) copy-start(f32[2,512,1024]{2,1,0:T(8,128)S(1)} %get-tuple-element.206) | copy-start | bytes 12582916
  559.3 42.4 %copy-start.49 = (f32[2,128,1024]{2,1,0:T(8,128)S(1)}, f32[2,128,1024]{2,1,0:T(8,128)}, u32[]{:S(2)}) copy-start(f32[2,128,1024]{2,1,0:T(8,128)} %convolution_bitcast_fusion.2) | copy-start | bytes 3145732
  559.3 42.4 %copy-start.73 = (bf16[1024,256]{1,0:T(8,128)(2,1)S(1)}, bf16[1024,256]{1,0:T(8,128)(2,1)}, u32[]{:S(2)}) copy-start(bf16[1024,256]{1,0:T(8,128)(2,1)} %param.24) | copy-start | bytes 1572868
  (123 other events, 349.5 us)
Sparse Core Ops, SparseCore 0:
  31.5 28.2 all-gather.10
  62.3 28.2 all-gather.6
  318.6 41.6 all-gather.12
  363.4 75.3 reduce-scatter.4
  441.6 78.3 reduce-scatter.2
  631.7 46.2 all-gather.8

commit v3 on v1

--- a/solution.py
+++ b/solution.py
@@ -261,6 +261,101 @@
         ],
         compiler_params=pltpu.CompilerParams(vmem_limit_bytes=48 * 1024 * 1024),
     )(low, high, query, grad, place, begin, stat, dots, keyval, keyval_t)
+
+
+def grads_kernel(ways, part_ref, out_ref, paired, landed, spread, sends, arrivals):
+    me = lax.axis_index("seq")
+    core = lax.rem(me, 2)
+    chips = ways // 2
+    chip = me // 2
+    sibling = me + 1 - 2 * core
+    half = part_ref.shape[0] // 2
+    share = half // chips
+    barrier = pltpu.get_barrier_semaphore()
+    peers = [lax.rem(chip + hop, chips) * 2 + core for hop in range(1, chips)]
+    for peer in peers + [sibling]:
+        pl.semaphore_signal(
+            barrier, inc=1, device_id={"seq": peer}, device_id_type=pl.DeviceIdType.MESH
+        )
+    pl.semaphore_wait(barrier, chips)
+
+    def send(source, target, number, peer):
+        copy = pltpu.make_async_remote_copy(
+            src_ref=source,
+            dst_ref=target,
+            send_sem=sends.at[number],
+            recv_sem=arrivals.at[number],
+            device_id={"seq": peer},
+            device_id_type=pl.DeviceIdType.MESH,
+        )
+        copy.start()
+        return copy
+
+    def span(start, size):
+        return pl.ds(pl.multiple_of(start, 16), size)
+
+    own = core * half
+    send(part_ref.at[span((1 - core) * half, half), :], landed, 0, sibling).wait()
+
+    @pl.loop(0, half // 16)
+    def _(tile):
+        here = span(tile * 16, 16)
+        paired[here, :] = (
+            part_ref[span(own + tile * 16, 16), :].astype(jnp.float32)
+            + landed[here, :].astype(jnp.float32)
+        ).astype(paired.dtype)
+
+    copies = []
+    for hop in range(1, chips):
+        to = lax.rem(chip + hop, chips)
+        copies.append(
+            send(paired.at[span(to * share, share), :], spread.at[hop - 1], hop, peers[hop - 1])
+        )
+    for copy in copies:
+        copy.wait()
+    mine = own + chip * share
+
+    @pl.loop(0, share // 16)
+    def _(tile):
+        here = span(tile * 16, 16)
+        total = paired[span(chip * share + tile * 16, 16), :].astype(jnp.float32)
+        for hop in range(1, chips):
+            total = total + spread[hop - 1, here, :].astype(jnp.float32)
+        out_ref[span(mine + tile * 16, 16), :] = total.astype(out_ref.dtype)
+
+    place = out_ref.at[span(mine, share), :]
+    copies = [
+        send(place, place, chips + hop, peers[hop - 1]) for hop in range(1, chips)
+    ]
+    for copy in copies:
+        copy.wait()
+    place = out_ref.at[span(own, half), :]
+    send(place, place, chips, sibling).wait()
+
+
+def grads_sum(part, number):
+    ways = lax.axis_size("seq")
+    rows, width = part.shape
+    chips = ways // 2
+    return pl.pallas_call(
+        partial(grads_kernel, ways),
+        out_shape=jax.ShapeDtypeStruct(part.shape, part.dtype),
+        in_specs=[pl.BlockSpec(memory_space=pltpu.VMEM)],
+        out_specs=pl.BlockSpec(memory_space=pltpu.VMEM),
+        scratch_shapes=[
+            pltpu.VMEM((rows // 2, width), part.dtype),
+            pltpu.VMEM((rows // 2, width), part.dtype),
+            pltpu.VMEM((chips - 1, rows // ways, width), part.dtype),
+            pltpu.SemaphoreType.DMA((2 * chips,)),
+            pltpu.SemaphoreType.DMA((2 * chips,)),
+        ],
+        cost_estimate=pl.CostEstimate(
+            flops=2 * part.size, bytes_accessed=48 * part.size, transcendentals=0
+        ),
+        compiler_params=pltpu.CompilerParams(
+            collective_id=number, has_side_effects=True, vmem_limit_bytes=32 * 1024 * 1024
+        ),
+    )(part)
 
 
 def local(
@@ -428,9 +523,21 @@
     middle_low_part = jnp.einsum(
         "rtkf,dkf->rtd", ffn_pre_grad, ffn_in, preferred_element_type=jnp.float32
     )
+    def tall(values):
+        return jnp.pad(values, ((0, model_width - values.shape[0]), (0, 0)))
+
+    early = jnp.concatenate(
+        [ffn_in_grad.reshape(model_width, -1), ffn_down_grad.T], axis=1
+    ).astype(jnp.bfloat16)
+    middle_low_part, early = lax.optimization_barrier(
+        (middle_low_part.astype(jnp.bfloat16), early)
+    )
     low_grad_share = lax.psum_scatter(
-        middle_low_part.astype(jnp.bfloat16), "head", scatter_dimension=1, tiled=True
-    ).astype(jnp.float32)
+        middle_low_part, "head", scatter_dimension=1, tiled=True
+    )
+    early_sum = grads_sum(early, 1)
+    low_grad_share, early_sum = lax.optimization_barrier((low_grad_share, early_sum))
+    low_grad_share = low_grad_share.astype(jnp.float32)
     norm_back_share, ffn_gain_part = norm_backward(
         low_grad_share, share_of(normed_two), share_of(scaled_two), ffn_gain
     )
@@ -594,45 +701,54 @@
         head_share + common_share, normed_share, share_of(scaled_one), norm_gain
     )
     token_share = (middle_grad_share + norm_back_share_one).astype(jnp.bfloat16)
+    small = [
+        step_proj_grad,
+        jnp.stack([ffn_gain_grad, norm_gain_grad], axis=1),
+        tall(conv_weight_grad[:, :inner_width].T),
+        tall(conv_weight_grad[:, inner_width:].T),
+        tall(jnp.stack([step_bias_grad, decay_log_grad, skip_gain_grad], axis=1)),
+    ]
+    small = jnp.concatenate(small, axis=1)
+    small = jnp.pad(small, ((0, 0), (0, 128 - small.shape[1])))
+    down_grads = [mixer_down_grad, attend_down_grad]
+    pieces = [
+        mixer_proj_grad.reshape(model_width, -1),
+        query_proj_grad,
+        state_proj_grad,
+        keyval_proj_grad.reshape(model_width, -1),
+        jnp.concatenate(down_grads, axis=0).T,
+        small,
+    ]
+    late = jnp.concatenate([piece.astype(jnp.bfloat16) for piece in pieces], axis=1)
+    token_share, late = lax.optimization_barrier((token_share, late))
     output, token_grad = (
         lax.all_gather(output_share, "head", axis=1, tiled=True),
         lax.all_gather(token_share, "head", axis=1, tiled=True),
     )
-    (
-        norm_gain_sum,
-        mixer_proj_sum,
-        state_proj_sum,
-        step_proj_sum,
-        step_bias_sum,
-        decay_log_sum,
-        skip_gain_sum,
-        conv_mixer_sum,
-        conv_state_sum,
-        mixer_down_sum,
-        query_proj_sum,
-        keyval_proj_sum,
-        attend_down_sum,
-        ffn_gain_sum,
-        ffn_in_sum,
-        ffn_down_sum,
-    ) = (
-        lax.psum(norm_gain_grad.astype(jnp.bfloat16), "seq").astype(jnp.float32),
-        lax.psum(mixer_proj_grad.astype(jnp.bfloat16), "seq").astype(jnp.float32),
-        lax.psum(state_proj_grad.astype(jnp.bfloat16), "seq").astype(jnp.float32),
-        lax.psum(step_proj_grad.astype(jnp.bfloat16), "seq").astype(jnp.float32),
-        lax.psum(step_bias_grad.astype(jnp.bfloat16), "seq").astype(jnp.float32),
-        lax.psum(decay_log_grad.astype(jnp.bfloat16), "seq").astype(jnp.float32),
-        lax.psum(skip_gain_grad.astype(jnp.bfloat16), "seq").astype(jnp.float32),
-        lax.psum(conv_weight_grad[:, :inner_width].astype(jnp.bfloat16), "seq").astype(jnp.float32),
-        lax.psum(conv_weight_grad[:, inner_width:].astype(jnp.bfloat16), "seq").astype(jnp.float32),
-        lax.psum(mixer_down_grad.astype(jnp.bfloat16), "seq").astype(jnp.float32),
-        lax.psum(query_proj_grad.astype(jnp.bfloat16), "seq").astype(jnp.float32),
-        lax.psum(keyval_proj_grad.astype(jnp.bfloat16), "seq").astype(jnp.float32),
-        lax.psum(attend_down_grad.astype(jnp.bfloat16), "seq").astype(jnp.float32),
-        lax.psum(ffn_gain_grad.astype(jnp.bfloat16), "seq").astype(jnp.float32),
-        lax.psum(ffn_in_grad.astype(jnp.bfloat16), "seq").astype(jnp.float32),
-        lax.psum(ffn_down_grad.astype(jnp.bfloat16), "seq").astype(jnp.float32),
-    )
+    summed = grads_sum(late, 2)
+    parts = []
+    begin = 0
+    for piece in pieces:
+        parts.append(summed[:, begin : begin + piece.shape[1]].astype(jnp.float32))
+        begin += piece.shape[1]
+    mixer_proj_sum = parts[0].reshape(mixer_proj_grad.shape)
+    query_proj_sum, state_proj_sum = parts[1], parts[2]
+    keyval_proj_sum = parts[3].reshape(keyval_proj_grad.shape)
+    down_sum = parts[4].T
+    mixer_down_sum, attend_down_sum = down_sum[:inner_width], down_sum[inner_width:]
+    early_wide = ffn_in_grad.shape[1] * ffn_in_grad.shape[2]
+    ffn_in_sum = early_sum[:, :early_wide].astype(jnp.float32).reshape(ffn_in_grad.shape)
+    ffn_down_sum = early_sum[:, early_wide:].astype(jnp.float32).T
+    small_sum = parts[5]
+    at = head_count
+    step_proj_sum = small_sum[:, :at]
+    ffn_gain_sum, norm_gain_sum = small_sum[:, at], small_sum[:, at + 1]
+    at += 2
+    conv_mixer_sum = small_sum[:inner_width, at : at + tap_count].T
+    at += tap_count
+    conv_state_sum = small_sum[: 2 * states, at : at + tap_count].T
+    at += tap_count
+    step_bias_sum, decay_log_sum, skip_gain_sum = (small_sum[:head_count, at + i] for i in range(3))
     return (
         output,
         token_grad,

time: 802 us -> 727 us (0.906)
  waiting for transfers between devices: 465 us -> 254 us
  Pallas kernels: 8.74 us -> 119 us
  local copies, waits for them, and re-layouts: 70.2 us -> 102 us
  blocking collectives: 56.3 us -> 30.9 us
  other arithmetic: 65.1 us -> 74.7 us
    psum x2 -> x1, waiting for transfers between devices: 159 us -> 33.5 us  [local(): lax.psum(keyval_part.astype(jnp.bfloat16), 'head').astype(jnp.float32)]
    pallas_call x0 -> x2, Pallas kernels: none -> 110 us  [grads_sum(): pl.pallas_call(partial(grads_kernel, ways), out_shape=jax.ShapeDtypeStruc...]
    reduce_scatter x1, waiting for transfers between devices: 42.9 us -> 0.02 us  [local(): lax.psum_scatter(middle_low_part, 'head', scatter_dimension=1, tiled=True)]
    all_gather x1, waiting for transfers between devices: 40.9 us -> 7 us  [local(): lax.all_gather(output_share, 'head', axis=1, tiled=True)]
    psum x1 -> x0, blocking collectives: 23.2 us -> none  [local(): lax.psum(norm_gain_grad.astype(jnp.bfloat16), 'seq').astype(jnp.float32)]
    reshape x0 -> x4, local copies, waits for them, and re-layouts: none -> 16.1 us  [the longest x1 6.58 us: local(): early_sum[:, :early_wide].astype(jnp.float32).reshape(ffn_in_grad.shape)]
    reshape x0 -> x3, other arithmetic: none -> 8.41 us  [the longest x1 4.05 us: local(): early_sum[:, :early_wide].astype(jnp.float32).reshape(ffn_in_grad.shape)]
    convert_element_type x13 -> x1, other arithmetic: 10.1 us -> 2.02 us  [local(): parts.append(summed[:, begin:begin + piece.shape[1]].astype(jnp.float32))]
  transfers between devices with their start and end apart: 15 -> 14, of which waited for: 11 -> 8; matrix products, arithmetic and copies ran while one was open for 20% -> 26% of each run, Pallas kernels for 1% -> 16%
where the time goes in v3:
time: 727 us; the launch traced here: 715 us
  waiting for transfers between devices  254 us (35%)
  Pallas kernels  119 us (16%)
  matrix products  113 us (16%)
  local copies, waits for them, and re-layouts  102 us (14%)
  other arithmetic  74.7 us (10%)
  blocking collectives  30.9 us (4%)
  between operations  16.3 us (2%)
    pallas_call x2, Pallas kernels, grads_sum(): pl.pallas_call(partial(grads_kernel, ways), out_shape=jax.ShapeDtypeStruc...  110 us
    psum x1, waiting for transfers between devices, local(): lax.psum((mixer_part + attend_part).astype(jnp.bfloat16), 'head')  96.3 us
    unnamed x311, local copies, waits for them, and re-layouts  52.5 us
    all_gather x1, waiting for transfers between devices, local(): lax.all_gather(middle_grad_share.astype(jnp.bfloat16), 'head', axis=1, ti...  44.1 us
    psum x1, waiting for transfers between devices, local(): lax.psum(keyval_part.astype(jnp.bfloat16), 'head').astype(jnp.float32)  33.5 us
    reduce_scatter x1, waiting for transfers between devices, local(): lax.psum_scatter(keyval_grads, 'seq', scatter_dimension=1, tiled=True)  24.2 us
    dot_general x3, matrix products, state_output(): jnp.einsum('rtsh,rshp->rthp', gram_mat[..., None] * decay_mat, drive_in,...  22.6 us
    all_gather x1, waiting for transfers between devices, local(): lax.all_gather(jnp.concatenate([key_rot, value_low], axis=2), 'seq', axis...  19.7 us
  transfers between devices with their start and end apart: 14, of which 8 were waited for; matrix products, arithmetic and copies ran while one was open for 26% of the time, Pallas kernels for 16%

profile of v3, /device:TPU:0, one launch (start us, length us, event | category | flops | bytes accessed | tf_op | source)
XLA Modules:
  0.0 714.7 jit_solution(8710662978178738022)
XLA Ops:
  9.4 5.0 copy.416
  29.2 4.5 multiply_convert_fusion.2
  49.8 13.2 %all_gather.28 = bf16[8,2,6]{2,1,0:T(2,128)(2,1)S(1)} all-gather(bf16[1,2,6]{2,1,0:T(2,128)(2,1)S(1)} %fusion.219), channel_id=1, replica_groups=mesh['seq'=8,'head'=4] {'seq'}, dimensions={0}, use_global_device_ids=true | all-gather | bytes 216 | tf_op jit(solution)/shard_map/all_gather | solution.py:448
  70.7 7.3 %multiply_convert_fusion.7 = (bf16[2,512,6,64]{1,3,2,0:T(8,128)(2,1)}, f32[2,512,6,64]{1,3,2,0:T(8,128)}) fusion(f32[2,512,6,64]{1,3,2,0:T(8,128)S(1)} %bitcast.434, f32[2,512,6,64]{1,3,2,0:T(8,128)S(1)} %bitcast.428, f32[6]{0:T(128)S(1)} %copy-done.136, f32[2,512,6,64]{1,3,2,0:T(8,128)S(1)} %fusion.145, f32[2,512,6]{1,2,0:T(8,128)S(1)} %copy-done.88, ...), kind=kOutput, calls=%fused_computation.127 | convolution fusion | flops 419561472 | bytes 9773080 | tf_op jit(solution)/shard_map/jvp(rtsh,rshp->rthp)/dot_general | solution.py:125
  77.9 19.7 %all-gather.9.cloned.1.call-done = bf16[2,4096,128]{1,2,0:T(8,128)(2,1)} async-done(((bf16[2,512,128]{1,2,0:T(8,128)(2,1)}), bf16[2,4096,128]{1,2,0:T(8,128)(2,1)}) %all-gather.9.cloned.1.call-update) | async-done | bytes 2097168 | tf_op jit(solution)/shard_map/all_gather | solution.py:475
  97.7 4.2 copy.433.kv_ref
  112.3 96.3 %all-reduce.18.cloned.1.call-done = bf16[2,512,1024]{2,1,0:T(8,128)(2,1)} async-done(((bf16[2,512,1024]{2,1,0:T(8,128)(2,1)}), bf16[2,512,1024]{2,1,0:T(8,128)(2,1)}) %all-reduce.18.cloned.1.call-update) | async-done | bytes 2097168 | tf_op jit(solution)/shard_map/psum | solution.py:497
  208.7 4.4 convert_add_fusion
  220.9 3.7 bitcast_convert_fusion
  224.6 3.7 bitcast_convert_fusion.1
  239.9 47.4 %shard_map.323 = bf16[1024,1536]{1,0:T(8,128)(2,1)S(1)} custom-call(bf16[1024,1536]{1,0:T(8,128)(2,1)S(1)} %copy-done.6), custom_call_target="tpu_custom_call" | custom-call | flops 3145728 | bytes 75497472 | tf_op jit(solution)/shard_map/pallas_call | solution.py:340
  294.1 44.1 %all-gather.13.cloned.1.call-done = bf16[2,512,1024]{2,1,0:T(8,128)(2,1)} async-done(((bf16[2,128,1024]{2,1,0:T(8,128)(2,1)}), bf16[2,512,1024]{2,1,0:T(8,128)(2,1)}) %all-gather.13.cloned.1.call-update) | async-done | bytes 2097168 | tf_op jit(solution)/shard_map/all_gather | solution.py:545
  338.2 4.1 fusion.68
  355.2 5.7 shard_map.324
  363.0 4.3 copy.457
  368.8 10.1 %fusion.11 = (f32[2,512,6]{1,2,0:T(8,128)}, f32[2,512,6]{1,2,0:T(8,128)}, bf16[2,512,512]{2,1,0:T(8,128)(2,1)S(1)}) fusion(f32[2,512,6]{1,2,0:T(8,128)S(1)} %bitcast.459, f32[2,512,512]{2,1,0:T(8,128)} %fusion.170, pred[2,512,512]{2,1,0:T(8,128)(4,1)} %compare_and_fusion, f32[2,512,6,64]{1,3,2,0:T(8,128)S(1)} %bitcast.429, ...), kind=kOutput, calls=%fused_computation.12 | convolution fusion | flops 437112832 | bytes 6914048 | tf_op jit(solution)/shard_map/transpose(jvp(rtsh,rshp->rthp))/dot_general | solution.py:125
  382.1 5.2 fusion.6
  398.0 24.2 %reduce-scatter.13.cloned.1.call-done = bf16[2,512,128]{1,2,0:T(8,128)(2,1)} async-done(((bf16[2,4096,128]{1,2,0:T(8,128)(2,1)}), bf16[2,512,128]{1,2,0:T(8,128)(2,1)}) %reduce-scatter.13.cloned.1.call-update) | async-done | bytes 262160 | tf_op jit(solution)/shard_map/reduce_scatter | solution.py:578
  425.0 3.8 convolution_convert_fusion
  441.0 3.6 fusion.201
  444.6 33.5 %all-reduce.20.cloned.1.call-done = (bf16[2,512,2,128]{3,1,2,0:T(8,128)(2,1)}, bf16[2,512,256]{1,2,0:T(8,128)(2,1)}) async-done(((bf16[2,512,2,128]{3,1,2,0:T(8,128)(2,1)}, bf16[2,512,256]{1,2,0:T(8,128)(2,1)}), (bf16[2,512,2,128]{3,1,2,0:T(8,128)(2,1)}, bf16[2,512,256]{1,2,0:T(8,128)(2,1)})) %all-reduce.20.cloned.1.call-update) | async-done | bytes 1048592 | tf_op jit(solution)/shard_map/psum | solution.py:625
  488.7 8.3 %pad_add_fusion = f32[2,515,640]{1,2,0:T(8,128)} fusion(f32[2,512,640]{1,2,0:T(8,128)} %copy-done.27, f32[2,512,640]{1,2,0:T(8,128)} %copy-done.26, f32[2,512,640]{1,2,0:T(8,128)} %copy-done.28, f32[2,512,640]{1,2,0:T(8,128)} %copy-done.25), kind=kLoop, calls=%fused_computation.36 | loop fusion | flops 1977600 | bytes 13122560 | tf_op jit(solution)/shard_map/add | solution.py:634
  502.2 6.9 multiply_reduce_fusion
  510.3 13.9 %reduce-scatter.7.cloned.1.call-done = bf16[2,128,1024]{2,1,0:T(8,128)(2,1)} async-done(((bf16[2,512,1024]{2,1,0:T(8,128)(2,1)}), bf16[2,128,1024]{2,1,0:T(8,128)(2,1)}) %reduce-scatter.7.cloned.1.call-update) | async-done | bytes 524304 | tf_op jit(solution)/shard_map/reduce_scatter | solution.py:506
  539.2 4.5 bitcast_convert_fusion.2
  555.8 14.5 %reduce-scatter.11.cloned.1.call-done = bf16[2,128,1024]{2,1,0:T(8,128)(2,1)} async-done(((bf16[2,512,1024]{2,1,0:T(8,128)(2,1)}), bf16[2,128,1024]{2,1,0:T(8,128)(2,1)}) %reduce-scatter.11.cloned.1.call-update) | async-done | bytes 524304 | tf_op jit(solution)/shard_map/reduce_scatter | solution.py:678
  573.4 17.7 %all-reduce.13 = (bf16[1,4,1024]{2,1,0:T(4,128)(2,1)S(1)}, bf16[1,4,1024]{2,1,0:T(4,128)(2,1)S(1)}) all-reduce(bf16[1,4,1024]{2,1,0:T(4,128)(2,1)S(1)} %broadcast_in_dim.305, bf16[1,4,1024]{2,1,0:T(4,128)(2,1)S(1)} %broadcast_in_dim.306), channel_id=8, replica_groups=mesh['seq'=8,'head'=4] {'head'}, use_global_device_ids=true, to_apply=%region_27.28.clone | all-reduce | flops 8192 | bytes 32768
  597.0 4.0 slice_convert_fusion
  601.0 6.6 reshape.572
  611.0 7.0 all-gather.11.cloned.1.call-done
  618.0 62.5 %shard_map.325 = bf16[1024,2048]{1,0:T(8,128)(2,1)S(1)} custom-call(bf16[1024,2048]{1,0:T(8,128)(2,1)} %pad_dynamic-update-slice_fusion.part_ref), custom_call_target="tpu_custom_call" | custom-call | flops 4194304 | bytes 100663296 | tf_op jit(solution)/shard_map/pallas_call | solution.py:340
  685.0 5.2 reshape.568
  (508 shorter events, 199.1 us)
Async XLA Ops:
  7.2 209.9 %copy-start = (bf16[512,1024]{1,0:T(8,128)(2,1)S(1)}, bf16[512,1024]{1,0:T(8,128)(2,1)}, u32[]{:S(2)}) copy-start(bf16[512,1024]{1,0:T(8,128)(2,1)} %param.37) | copy-start | bytes 3145732
  7.2 59.9 %all-gather.17.cloned.1.call-start = ((), (), s32[]{:S(2)}) async-start(), calls=%async_computation.13 | async-start | bytes 1769472 | tf_op jit(solution)/shard_map/all_gather | solution.py:450
  21.5 6.7 collective-permute-start
  25.8 341.8 %copy-start.79 = (f32[2,512,6]{1,2,0:T(8,128)}, f32[2,512,6]{1,2,0:T(8,128)S(1)}, u32[]{:S(2)}) copy-start(f32[2,512,6]{1,2,0:T(8,128)S(1)} %add_select_fusion) | copy-start | bytes 73732
  36.4 61.2 %all-gather.9.cloned.1.call-start = ((), (), s32[]{:S(2)}) async-start(), calls=%async_computation.4 | async-start | bytes 2359296 | tf_op jit(solution)/shard_map/all_gather | solution.py:475
  42.6 166.1 %all-reduce.18.cloned.1.call-start = ((), (), s32[]{:S(2)}) async-start(), calls=%async_computation.5 | async-start | bytes 4194304 | tf_op jit(solution)/shard_map/psum | solution.py:497
  48.6 16.7 %copy-start.33 = (bf16[2,512,640]{1,2,0:T(8,128)(2,1)S(1)}, bf16[2,512,640]{1,2,0:T(8,128)(2,1)}, u32[]{:S(2)}) copy-start(bf16[2,512,640]{1,2,0:T(8,128)(2,1)} %copy-done.32) | copy-start | bytes 3932164
  111.9 96.8 %copy-start.17 = (bf16[2,512,1024]{2,1,0:T(8,128)(2,1)S(1)}, bf16[2,512,1024]{2,1,0:T(8,128)(2,1)}, u32[]{:S(2)}) copy-start(bf16[2,512,1024]{2,1,0:T(8,128)(2,1)} %param.19) | copy-start | bytes 6291460
  111.9 177.1 %reduce-scatter.9.cloned.1.call-start = ((), (), s32[]{:S(2)}) async-start(), calls=%async_computation.8 | async-start | bytes 2621440 | tf_op jit(solution)/shard_map/reduce_scatter | solution.py:535
  237.8 100.4 %all-gather.13.cloned.1.call-start = ((), (), s32[]{:S(2)}) async-start(), calls=%async_computation.9 | async-start | bytes 2621440 | tf_op jit(solution)/shard_map/all_gather | solution.py:545
  289.0 49.2 %copy-start.34 = (bf16[2,512,640]{1,2,0:T(8,128)(2,1)S(1)}, bf16[2,512,640]{1,2,0:T(8,128)(2,1)}, u32[]{:S(2)}) copy-start(bf16[2,512,640]{1,2,0:T(8,128)(2,1)} %copy-done.32) | copy-start | bytes 3932164
  289.0 49.2 %copy-start.75 = (bf16[384,1024]{1,0:T(8,128)(2,1)S(1)}, bf16[384,1024]{1,0:T(8,128)(2,1)}, u32[]{:S(2)}) copy-start(bf16[384,1024]{1,0:T(8,128)(2,1)} %param.31) | copy-start | bytes 2359300
  291.4 50.9 %copy-start.125 = (f32[2,128]{1,0:T(2,128)}, f32[2,128]{1,0:T(2,128)S(1)}, u32[]{:S(2)}) copy-start(f32[2,128]{1,0:T(2,128)S(1)} %broadcast_multiply_fusion.4) | copy-start | bytes 3076
  294.1 93.3 %all-gather.19.cloned.1.call-start = ((), (), s32[]{:S(2)}) async-start(), calls=%async_computation.14 | async-start | bytes 1769472 | tf_op jit(solution)/shard_map/all_gather | solution.py:604
  347.1 75.1 %reduce-scatter.13.cloned.1.call-start = ((), (), s32[]{:S(2)}) async-start(), calls=%async_computation.11 | async-start | bytes 2359296 | tf_op jit(solution)/shard_map/reduce_scatter | solution.py:578
  367.4 110.8 %all-reduce.20.cloned.1.call-start = ((), (), s32[]{:S(2)}) async-start(), calls=%async_computation.15 | async-start | bytes 2097152 | tf_op jit(solution)/shard_map/psum | solution.py:625
  397.1 26.2 %copy-start.133 = (f32[32]{0:T(128)S(1)}, f32[32]{0:T(128)}, u32[]{:S(2)}) copy-start(f32[32]{0:T(128)} %copy-done.132) | copy-start | bytes 388
  425.0 99.3 %reduce-scatter.7.cloned.1.call-start = ((), (), s32[]{:S(2)}) async-start(), calls=%async_computation.6 | async-start | bytes 2621440 | tf_op jit(solution)/shard_map/reduce_scatter | solution.py:506
  428.8 141.4 %reduce-scatter.11.cloned.1.call-start = ((), (), s32[]{:S(2)}) async-start(), calls=%async_computation.10 | async-start | bytes 2621440 | tf_op jit(solution)/shard_map/reduce_scatter | solution.py:678
  441.0 38.3 %copy-start.98 = (f32[640]{0:T(1024)S(1)}, f32[640]{0:T(1024)}, u32[]{:S(2)}) copy-start(f32[640]{0:T(1024)} %copy-done.97) | copy-start | bytes 7684
  441.0 38.3 %copy-start.100 = (f32[640]{0:T(1024)S(1)}, f32[640]{0:T(1024)}, u32[]{:S(2)}) copy-start(f32[640]{0:T(1024)} %copy-done.99) | copy-start | bytes 7684
  441.0 38.3 %copy-start.110 = (pred[2,512]{1,0:T(4,128)(4,1)S(1)}, pred[2,512]{1,0:T(4,128)(4,1)}, u32[]{:S(2)}) copy-start(pred[2,512]{1,0:T(4,128)(4,1)} %copy-done.109) | copy-start | bytes 3076
  441.0 38.3 %copy-start.112 = (pred[2,512]{1,0:T(4,128)(4,1)S(1)}, pred[2,512]{1,0:T(4,128)(4,1)}, u32[]{:S(2)}) copy-start(pred[2,512]{1,0:T(4,128)(4,1)} %copy-done.111) | copy-start | bytes 3076
  487.4 9.6 %collective-permute-start.1 = (f32[2,3,640]{2,0,1:T(2,128)S(1)}, f32[2,3,640]{2,0,1:T(2,128)S(1)}, u32[]{:S(2)}, u32[]{:S(2)}) collective-permute-start(f32[2,3,640]{2,0,1:T(2,128)S(1)} %copy.446), channel_id=1, source_target_pairs={{4,0},{8,4},{12,8},{16,12},{20,16},{24,20},{28,24},{5,1},{9,5},{13... | collective-permute-start | bytes 46088 | tf_op jit(solution)/shard_map/ppermute | solution.py:26
  509.1 17.8 %copy-start.135 = (f32[384]{0:T(512)S(1)}, f32[384]{0:T(512)}, u32[]{:S(2)}) copy-start(f32[384]{0:T(512)} %get-tuple-element.249) | copy-start | bytes 4612
  509.1 18.0 %copy-start.61 = (bf16[2,8,2,8,512]{4,3,1,2,0:T(8,128)(2,1)S(1)}, bf16[2,8,2,8,512]{4,3,1,2,0:T(8,128)(2,1)}, u32[]{:S(2)}) copy-start(bf16[2,8,2,8,512]{4,3,1,2,0:T(8,128)(2,1)} %copy-done.60) | copy-start | bytes 786436
  509.1 108.8 %all-gather.11.cloned.1.call-start = ((), (), s32[]{:S(2)}) async-start(), calls=%async_computation.7 | async-start | bytes 2621440 | tf_op jit(solution)/shard_map/all_gather | solution.py:725
  526.6 176.5 %all-gather.15.cloned.1.call-start = ((), (), s32[]{:S(2)}) async-start(), calls=%async_computation.12 | async-start | bytes 2621440 | tf_op jit(solution)/shard_map/all_gather | solution.py:726
  554.6 15.7 %copy-start.57 = (f32[2,128,1024]{2,1,0:T(8,128)S(1)}, f32[2,128,1024]{2,1,0:T(8,128)}, u32[]{:S(2)}) copy-start(f32[2,128,1024]{2,1,0:T(8,128)} %convolution_bitcast_fusion.2) | copy-start | bytes 3145732
  570.3 23.1 %copy-start.54 = (bf16[2,128,1024]{2,1,0:T(8,128)(2,1)S(1)}, bf16[2,128,1024]{2,1,0:T(8,128)(2,1)}, u32[]{:S(2)}) copy-start(bf16[2,128,1024]{2,1,0:T(8,128)(2,1)} %reduce-scatter.9.cloned.1.call-done) | copy-start | bytes 1572868
  570.3 23.1 %copy-start.124 = (f32[2,128]{1,0:T(2,128)S(1)}, f32[2,128]{1,0:T(2,128)}, u32[]{:S(2)}) copy-start(f32[2,128]{1,0:T(2,128)} %copy-done.123) | copy-start | bytes 3076
  570.3 23.1 %copy-start.126 = (f32[2,128]{1,0:T(2,128)S(1)}, f32[2,128]{1,0:T(2,128)}, u32[]{:S(2)}) copy-start(f32[2,128]{1,0:T(2,128)} %copy-done.125) | copy-start | bytes 3076
  (133 other events, 433.9 us)
Sparse Core Ops, SparseCore 0:
  36.5 30.3 all-gather.16
  69.4 28.1 all-gather.8
  112.0 96.6 all-reduce.17
  237.9 42.7 reduce-scatter.8
  294.2 43.9 all-gather.12
  347.2 24.3 all-gather.18
  375.5 46.6 reduce-scatter.12
  425.9 52.1 all-reduce.19
  481.0 43.2 reduce-scatter.6
  527.1 43.1 reduce-scatter.10
  572.4 45.4 all-gather.10
  619.9 44.7 all-gather.14
